TPU v7x, 256 devices: a whole 4x4x8 slice. The times are simulated.
256 devices in a mesh: row: 8 (over x, z_lo), col: 32 (over y, z_hi, core).
Axes of the slice: x: 4, y: 4, z: 8 (z_hi: 4, z_lo: 2; z = z_hi * 2 + z_lo), core: 2. Of those that a mesh axis runs over, the one named last changes fastest.
Arguments:
- features: bfloat16 [262144, 128], P(('row', 'col')), may hold values from -6 to 6
- tiles: bfloat16 [8, 32, 368, 128, 128], P('row', 'col'), may hold values from -0.078125 to 0.078125
- tile_rows: int32 [8, 32, 368], P('row', 'col'), may hold values from 0 to 255
- tile_cols: int32 [8, 32, 368], P('row', 'col'), may hold values from 0 to 63
- tile_count: int32 [8, 32], P('row', 'col'), may hold values from 92 to 368, as said below
- weight: bfloat16 [128, 128], replicated, may hold values from -0.5 to 0.5
- bias: float32 [128], replicated, may hold values from -3 to 3
- cotangent: bfloat16 [262144, 128], P(('row', 'col')), may hold values from -6 to 6
Outputs:
- activations: bfloat16 [262144, 128], P(('row', 'col'))
- grad_features: bfloat16 [262144, 128], P(('row', 'col'))
- grad_weight: float32 [128, 128], replicated
- grad_bias: float32 [128], replicated
Inputs may be any that keep to these rules, and one draw needn't show every extreme that they name: `tile_count`: live slots of one grid cell; some cell has all 368 live.
All inputs are finite; a program needn't handle non-finite values.
Results may differ from a plain program's by a relative error of at most 0.0059.
Values may be sent and summed in bfloat16 or wider, within the bound.
No kernel may reach another device: no remote copies, remote signals or barrier semaphores. Data moves between devices by JAX's collectives and lax.ppermute only.
A program may use at most 128 MiB of HBM per device.

v0:
```python
import functools

import jax
import jax.numpy as jnp
from jax import lax
from jax.experimental import pallas as pl
from jax.experimental.pallas import tpu as pltpu
from jax.sharding import PartitionSpec as P

NX, NZL, NY, NZH, NCO = 4, 2, 4, 4, 2
EDGE = 128
PARTS = (4, 4)
AREAS = tuple(NY * NZH * tiles for tiles in PARTS)
TERMS = EDGE + 16
BLOCK0 = PARTS[0] * EDGE + TERMS
BLOCK1 = PARTS[1] * EDGE + TERMS + 16
SENT = 8 * EDGE + TERMS
GROUP = 8
SLOTS = 384
VMEM = 64 * 1024 * 1024 - 64 * 1024
BF = jnp.bfloat16
F32 = jnp.float32


def moved(index, count, step):
    return (index + step) % count


def row_perm(dx=0, dzl=0):
    return [
        (x * NZL + z, moved(x, NX, dx) * NZL + moved(z, NZL, dzl))
        for x in range(NX)
        for z in range(NZL)
    ]


def col_perm(dy=0, dzh=0, dco=0):
    return [
        (
            (y * NZH + z) * NCO + c,
            (moved(y, NY, dy) * NZH + moved(z, NZH, dzh)) * NCO + moved(c, NCO, dco),
        )
        for y in range(NY)
        for z in range(NZH)
        for c in range(NCO)
    ]


def send_row(value, **step):
    return lax.ppermute(value, "row", row_perm(**step))


def send_col(value, **step):
    return lax.ppermute(value, "col", col_perm(**step))


def in_smem():
    return pl.BlockSpec(memory_space=pltpu.SMEM)


def in_vmem():
    return pl.BlockSpec(memory_space=pltpu.VMEM)


def in_any():
    return pl.BlockSpec(memory_space=pl.ANY)


def shape_of(rows, dtype):
    return jax.ShapeDtypeStruct((rows, EDGE), dtype)


def params():
    return pltpu.CompilerParams(vmem_limit_bytes=VMEM)


def slot_entries(row_tiles, col_tiles):
    row, col = lax.axis_index("row"), lax.axis_index("col")
    my_x, my_zl = row >> 1, row & 1
    my_y, my_zh, my_co = col >> 3, (col >> 1) & 3, col & 1
    owner, inner = row_tiles >> 3, row_tiles & 7
    dy = ((owner >> 3) - my_y) & 3
    dz = (((owner >> 1) & 3) - my_zh) & 3
    other = (owner & 1) ^ my_co
    later = inner >= PARTS[0]
    part = later.astype(jnp.int32) * 2 + other
    ring = dy * NZH + dz
    row_place = jnp.where(later, ring * PARTS[1] + inner - PARTS[0], ring * PARTS[0] + inner)
    source = jnp.where(
        later,
        (NY * NZH * NCO * BLOCK0 + TERMS + 16) // 16
        + (other * NY * NZH + ring) * (BLOCK1 // 16)
        + (inner - PARTS[0]) * (EDGE // 16),
        owner * (BLOCK0 // 16) + inner * (EDGE // 16),
    )
    backward = col_tiles | (source << 7)
    owner, inner = col_tiles >> 3, col_tiles & 7
    dx = ((owner >> 1) - my_x) & 3
    col_place = (dx * 2 + ((owner & 1) ^ my_zl)) * 8 + inner
    slot = lax.broadcasted_iota(jnp.int32, row_tiles.shape, row_tiles.ndim - 1)
    return part, slot | (col_place << 9) | (row_place << 16), backward


def bins_kernel(count_ref, part_ref, entry_ref, list_ref, number_ref):
    for part in range(4):
        number_ref[part] = 0

    def one(slot, carry):
        part = part_ref[slot]
        at = number_ref[part]
        list_ref[part * SLOTS + at] = entry_ref[slot]
        number_ref[part] = at + 1
        return carry

    count = count_ref[0, 0]
    number_ref[4] = count
    lax.fori_loop(0, count, one, 0)
    for part in range(4):
        last = number_ref[part]
        for extra in range(GROUP - 1):
            list_ref[part * SLOTS + last + extra] = 64 << 9


def make_bins(count, part, entry):
    return pl.pallas_call(
        bins_kernel,
        out_shape=(
            jax.ShapeDtypeStruct((4 * SLOTS,), jnp.int32),
            jax.ShapeDtypeStruct((8,), jnp.int32),
        ),
        in_specs=[in_smem()] * 3,
        out_specs=(in_smem(),) * 2,
        compiler_params=params(),
        name="bins",
    )(count, part, entry)


def groups_of(number_ref, part):
    return (number_ref[part] + (GROUP - 1)) // GROUP


def start_tiles(list_ref, tiles_ref, buffer, sems, part, groups, first_group):
    def issue(group, carry):
        for k in range(GROUP):
            entry = list_ref[part * SLOTS + group * GROUP + k]
            pltpu.make_async_copy(
                tiles_ref.at[entry & 511],
                buffer.at[(first_group + group) * GROUP + k],
                sems.at[first_group + group],
            ).start()
        return carry

    lax.fori_loop(0, groups, issue, 0)


def wait_group(tiles_ref, buffer, sems, group):
    pltpu.make_async_copy(
        tiles_ref.at[pl.ds(0, GROUP)],
        buffer.at[pl.ds(group * GROUP, GROUP)],
        sems.at[group],
    ).wait()


def place(index):
    return pl.ds(pl.multiple_of(index * EDGE, EDGE), EDGE)


BATCH = 4


def forward_sum(part, list_ref, number_ref, pieces, tiles_ref, xbuf, tbuf, acc, xsem, tsem, start):
    groups = groups_of(number_ref, part)
    copies = [
        pltpu.make_async_copy(piece, xbuf.at[pl.ds(k * 1024, 1024)], xsem.at[k])
        for k, piece in enumerate(pieces)
    ]
    for copy in copies:
        copy.start()
    start_tiles(list_ref, tiles_ref, tbuf, tsem, part, groups, 0)
    start()
    xbuf[pl.ds(64 * EDGE, EDGE), :] = jnp.zeros((EDGE, EDGE), BF)
    for copy in copies:
        copy.wait()

    def body(group, carry):
        wait_group(tiles_ref, tbuf, tsem, group)
        for first in range(0, GROUP, BATCH):
            entries = [
                list_ref[part * SLOTS + group * GROUP + first + k] for k in range(BATCH)
            ]
            products = [
                jnp.dot(
                    tbuf[group * GROUP + first + k],
                    xbuf[place((entry >> 9) & 127), :],
                    preferred_element_type=F32,
                )
                for k, entry in enumerate(entries)
            ]
            for entry, product in zip(entries, products):
                acc[place(entry >> 16), :] += product
        return carry

    lax.fori_loop(0, groups, body, 0)


def over_tiles(count, step):
    def one(index, carry):
        step(place(index))
        return carry

    lax.fori_loop(0, count, one, 0)


def forward_send_kernel(part, list_ref, number_ref, *refs):
    pieces, (tiles_ref, out_ref, xbuf, tbuf, acc, xsem, tsem) = refs[:8], refs[8:]

    def start():
        def clear(at):
            acc[at, :] = jnp.zeros((EDGE, EDGE), F32)

        over_tiles(AREAS[part], clear)

    forward_sum(2 * part + 1, list_ref, number_ref, pieces, tiles_ref, xbuf, tbuf, acc, xsem, tsem, start)

    def store(at):
        out_ref[at, :] = acc[at, :].astype(BF)

    over_tiles(AREAS[part], store)


def forward_keep_kernel(part, list_ref, number_ref, *refs):
    pieces, refs = refs[:8], refs[8:]
    tiles_ref, got_ref, own, to_right, to_left, rest_right, rest_left, xbuf, tbuf, acc, xsem, tsem = refs

    def start():
        def load(at):
            acc[at, :] = got_ref[at, :].astype(F32)

        over_tiles(AREAS[part], load)

    forward_sum(2 * part, list_ref, number_ref, pieces, tiles_ref, xbuf, tbuf, acc, xsem, tsem, start)
    split_relay(lambda k, rows: acc[pl.ds(k, rows), :], own, to_right, to_left, rest_right, rest_left)


def split_relay(read, own, to_right, to_left, rest_right, rest_left):
    block = own.shape[0]
    half = block // 2
    for k in range(0, half, 64):
        at, low = pl.ds(k, 64), pl.ds(half + k, 64)
        own[at, :] = read(k, 64)
        own[low, :] = read(half + k, 64)
        to_right[at, :] = read(2 * block + k, 64).astype(BF)
        to_right[low, :] = read(block + half + k, 64).astype(BF)
        to_left[at, :] = read(2 * block + half + k, 64).astype(BF)
        to_left[low, :] = read(3 * block + k, 64).astype(BF)
        rest_right[at, :] = read(block + k, 64)
        rest_left[at, :] = read(3 * block + half + k, 64)


def relay_shapes(block):
    half = block // 2
    return (shape_of(block, F32),) + (shape_of(block, BF),) * 2 + (shape_of(half, F32),) * 2


def forward_scratch(part):
    return [
        pltpu.VMEM((65 * EDGE, EDGE), BF),
        pltpu.VMEM((SLOTS, EDGE, EDGE), BF),
        pltpu.VMEM((AREAS[part] * EDGE, EDGE), F32),
        pltpu.SemaphoreType.DMA((8,)),
        pltpu.SemaphoreType.DMA((SLOTS // GROUP,)),
    ]


def forward_send(part, lists, numbers, pieces, tiles):
    return pl.pallas_call(
        functools.partial(forward_send_kernel, part),
        out_shape=shape_of(AREAS[part] * EDGE, BF),
        in_specs=[in_smem()] * 2 + [in_any()] * 9,
        out_specs=in_vmem(),
        scratch_shapes=forward_scratch(part),
        compiler_params=params(),
        name="forward_send",
    )(lists, numbers, *pieces, tiles)


def forward_keep(part, lists, numbers, pieces, tiles, got):
    return pl.pallas_call(
        functools.partial(forward_keep_kernel, part),
        out_shape=relay_shapes(AREAS[part] * EDGE // 4),
        in_specs=[in_smem()] * 2 + [in_any()] * 9 + [in_vmem()],
        out_specs=(in_vmem(),) * 5,
        scratch_shapes=forward_scratch(part),
        compiler_params=params(),
        name="forward_keep",
    )(lists, numbers, *pieces, tiles, got)


def relay_total(own, from_left, from_right, late_left, late_right):
    half = late_left.shape[0]

    def read(k, rows):
        at = pl.ds(k, rows)
        if k < half:
            return own[at, :] + from_right[pl.ds(half + k, rows), :].astype(F32) + late_left[at, :].astype(F32)
        return own[at, :] + from_left[at, :].astype(F32) + late_right[pl.ds(k - half, rows), :].astype(F32)

    return read


def middle_kernel(rest_right, rest_left, from_left, from_right, on_right, on_left):
    half = rest_right.shape[0]
    on_right[...] = (rest_right[...] + from_left[pl.ds(0, half), :].astype(F32)).astype(BF)
    on_left[...] = (rest_left[...] + from_right[pl.ds(0, half), :].astype(F32)).astype(BF)


def relay_middle(rest_right, rest_left, from_left, from_right):
    return pl.pallas_call(
        middle_kernel,
        out_shape=(shape_of(rest_right.shape[0], BF),) * 2,
        in_specs=[in_vmem()] * 4,
        out_specs=(in_vmem(),) * 2,
        compiler_params=params(),
        name="middle",
    )(rest_right, rest_left, from_left, from_right)


def turn_kernel(*refs):
    split_relay(relay_total(*refs[:5]), *refs[5:])


def ring_turn(*values):
    return pl.pallas_call(
        turn_kernel,
        out_shape=relay_shapes(values[0].shape[0] // 4),
        in_specs=[in_vmem()] * 5,
        out_specs=(in_vmem(),) * 5,
        compiler_params=params(),
        name="turn",
    )(*values)


def join_kernel(count, *refs):
    pieces, out_ref = refs[:count], refs[count]
    at = 0
    for piece in pieces:
        out_ref[pl.ds(at, piece.shape[0]), :] = piece[...]
        at += piece.shape[0]


def join(pieces):
    return pl.pallas_call(
        functools.partial(join_kernel, len(pieces)),
        out_shape=shape_of(sum(p.shape[0] for p in pieces), BF),
        in_specs=[in_vmem()] * len(pieces),
        out_specs=in_vmem(),
        compiler_params=params(),
        name="join",
    )(*pieces)


def dense_kernel(chunk, *refs):
    sums, (weight_ref, bias_ref, cot_ref), outs = refs[:5], refs[5:8], refs[8:]
    rows = PARTS[chunk] * EDGE
    skip = chunk * PARTS[0] * EDGE
    read = relay_total(*sums)
    hidden = jnp.concatenate([read(k, rows // 2).astype(BF) for k in (0, rows // 2)], axis=0)
    weight = weight_ref[...]
    pre = jnp.dot(hidden, weight, preferred_element_type=F32) + bias_ref[...]
    sigma = jax.nn.sigmoid(pre)
    act = (pre * sigma).astype(BF)
    if chunk:
        act_in, (act_ref, block_ref) = outs[0], outs[1:]
        act_ref[pl.ds(0, skip), :] = act_in[...]
        act_ref[pl.ds(skip, rows), :] = act
        terms_at, back_at = 0, TERMS + 16
        block_ref[pl.ds(TERMS, 16), :] = jnp.zeros((16, EDGE), BF)
    else:
        act_ref, block_ref = outs
        act_ref[...] = act
        terms_at, back_at = rows, 0
    grad_pre = cot_ref[pl.ds(skip, rows), :].astype(F32) * sigma * (1.0 + pre * (1.0 - sigma))
    grad_round = grad_pre.astype(BF)
    weight_term = lax.dot_general(hidden, grad_round, (((0,), (0,)), ((), ())), preferred_element_type=F32)
    bias_term = jnp.broadcast_to(jnp.sum(grad_pre, axis=0, keepdims=True), (16, EDGE))
    block_ref[pl.ds(terms_at, EDGE), :] = weight_term.astype(BF)
    block_ref[pl.ds(terms_at + EDGE, 16), :] = bias_term.astype(BF)
    for tile in range(PARTS[chunk]):
        part = grad_round[tile * EDGE : (tile + 1) * EDGE, :]
        back = lax.dot_general(weight, part, (((1,), (1,)), ((), ())), preferred_element_type=F32)
        block_ref[pl.ds(back_at + tile * EDGE, EDGE), :] = back.astype(BF)


def dense(chunk, sums, weight, bias, cotangent, before):
    return pl.pallas_call(
        functools.partial(dense_kernel, chunk),
        out_shape=(
            shape_of(sum(PARTS[: chunk + 1]) * EDGE, BF),
            shape_of((BLOCK0, BLOCK1)[chunk], BF),
        ),
        in_specs=[in_vmem()] * (8 + len(before)),
        out_specs=(in_vmem(),) * 2,
        compiler_params=params(),
        name="dense",
    )(*sums, weight, bias, cotangent, *before)


def both_ways(values):
    return (values[0] + values[2]) + (values[1] + values[3])


def backward_kernel(sizes, back_ref, number_ref, *refs):
    count = len(sizes)
    sources, tiles_ref = refs[:count], refs[count]
    out_ref, gbuf, tbuf, acc, gsem, tsem = refs[count + 1 :]
    groups = (number_ref[4] + (GROUP - 1)) // GROUP
    slots = tiles_ref.shape[0]
    copies, at = [], 0
    for k, size in enumerate(sizes):
        copies.append(pltpu.make_async_copy(sources[k], gbuf.at[pl.ds(at, size)], gsem.at[k]))
        at += size
    for copy in copies:
        copy.start()

    def tile_copy(group):
        at = pl.ds(group * GROUP, GROUP)
        return pltpu.make_async_copy(tiles_ref.at[at], tbuf.at[at], tsem.at[group])

    def issue(group, carry):
        tile_copy(group).start()
        return carry

    lax.fori_loop(0, groups, issue, 0)

    def clear(at):
        acc[at, :] = jnp.zeros((EDGE, EDGE), F32)

    over_tiles(65, clear)
    for copy in copies:
        copy.wait()

    def entry_of(slot):
        return jnp.where(slot < number_ref[4], back_ref[jnp.minimum(slot, slots - 1)], 64)

    def body(group, carry):
        tile_copy(group).wait()
        for first in range(0, GROUP, BATCH):
            entries = [entry_of(group * GROUP + first + k) for k in range(BATCH)]
            products = [
                jnp.dot(
                    gbuf[pl.ds(pl.multiple_of((entry >> 7) * 16, 16), EDGE), :],
                    tbuf[group * GROUP + first + k],
                    preferred_element_type=F32,
                )
                for k, entry in enumerate(entries)
            ]
            for entry, product in zip(entries, products):
                acc[place(entry & 127), :] += product
        return carry

    lax.fori_loop(0, groups, body, 0)

    second = NY * NZH * NCO * BLOCK0

    def terms_of(k, rows):
        total = jnp.zeros((rows, EDGE), F32)
        for owner in range(NY * NZH * NCO):
            total += gbuf[pl.ds(owner * BLOCK0 + PARTS[0] * EDGE + k, rows), :].astype(F32)
        cores = []
        for core in range(NCO):
            rings = []
            for dy in range(NY):
                first = second + (core * NY + dy) * NZH * BLOCK1 + k
                rings.append(
                    both_ways(
                        [gbuf[pl.ds(first + dz * BLOCK1, rows), :].astype(F32) for dz in range(NZH)]
                    )
                )
            cores.append(both_ways(rings))
        return (total + (cores[0] + cores[1])).astype(BF)

    for k in range(0, TERMS, 48):
        terms = terms_of(k, 48)
        for owner in range(8):
            out_ref[pl.ds(owner * SENT + 8 * EDGE + k, 48), :] = terms
    for owner in range(8):
        for tile in range(8):
            at = pl.ds(owner * SENT + tile * EDGE, EDGE)
            out_ref[at, :] = acc[pl.ds((owner * 8 + tile) * EDGE, EDGE), :].astype(BF)


def backward(backs, numbers, sources, tiles):
    sizes = tuple(source.shape[0] for source in sources)
    return pl.pallas_call(
        functools.partial(backward_kernel, sizes),
        out_shape=shape_of(8 * SENT, BF),
        in_specs=[in_smem()] * 2 + [in_any()] * (len(sizes) + 1),
        out_specs=in_vmem(),
        scratch_shapes=[
            pltpu.VMEM((sum(sizes), EDGE), BF),
            pltpu.VMEM((tiles.shape[0], EDGE, EDGE), BF),
            pltpu.VMEM((65 * EDGE, EDGE), F32),
            pltpu.SemaphoreType.DMA((len(sizes),)),
            pltpu.SemaphoreType.DMA((SLOTS // GROUP,)),
        ],
        compiler_params=params(),
        name="backward",
    )(backs, numbers, *sources, tiles)


def last_kernel(got_ref, out_ref, weight_ref, bias_ref):
    for tile in range(8):
        total = jnp.zeros((EDGE, EDGE), F32)
        for peer in range(8):
            total += got_ref[pl.ds(peer * SENT + tile * EDGE, EDGE), :].astype(F32)
        out_ref[pl.ds(tile * EDGE, EDGE), :] = total.T.astype(BF)
    terms = jnp.zeros((TERMS, EDGE), F32)
    for peer in range(8):
        terms += got_ref[pl.ds(peer * SENT + 8 * EDGE, TERMS), :].astype(F32)
    weight_ref[...] = terms[:EDGE]
    bias_ref[...] = terms[EDGE : EDGE + 1]


def last(got):
    return pl.pallas_call(
        last_kernel,
        out_shape=(shape_of(8 * EDGE, BF), shape_of(EDGE, F32), shape_of(1, F32)),
        in_specs=[in_vmem()],
        out_specs=(in_vmem(),) * 3,
        compiler_params=params(),
        name="last",
    )(got)


def after(value, *others):
    return lax.optimization_barrier((value, *others))[0]


def around(block, axis):
    half = block.shape[0] // 2
    left, right = send_col(block, **{axis: 1}), send_col(block, **{axis: -1})
    return right, send_col(left[:half], **{axis: 1}), send_col(right[half:], **{axis: -1}), left


def on_device(features, tiles, tile_rows, tile_cols, tile_count, weight, bias, cotangent):
    tile_set = tiles[0, 0]
    part, entry, backs = slot_entries(tile_rows[0, 0], tile_cols[0, 0])

    mine = features
    beside = after(send_row(mine, dzl=1), entry)
    mine_left, mine_right = send_row(mine, dx=1), send_row(mine, dx=-1)
    beside_left, beside_right = send_row(beside, dx=1), send_row(beside, dx=-1)
    mine_far = send_row(mine_left, dx=1)
    beside_far = send_row(beside_right, dx=-1)
    pieces = (mine, beside, mine_right, beside_right, mine_far, beside_far, mine_left, beside_left)
    lists, numbers = make_bins(after(tile_count, mine_left, beside_right), part, entry)

    latest = []

    def gate(value):
        return after(value, *latest) if latest else value

    def ran(values):
        latest[:] = [values[0]]
        return values

    both = (0, 1)
    got = []
    for c in both:
        (part,) = ran([forward_send(c, gate(lists), numbers, pieces, tile_set)])
        got.append(send_col(part, dco=1))
    rings = []
    for c in both:
        rings.append(ran(forward_keep(c, gate(lists), numbers, pieces, tile_set, got[c])))
    bias_row = bias.reshape(1, EDGE)
    for axis in ("dy", "dzh"):
        early = [(send_col(r[1], **{axis: 1}), send_col(r[2], **{axis: -1})) for r in rings]
        late = []
        for c in both:
            on_right, on_left = ran(relay_middle(gate(rings[c][3]), rings[c][4], *early[c]))
            late.append((send_col(on_right, **{axis: 1}), send_col(on_left, **{axis: -1})))
        sums = [(rings[c][0],) + early[c] + late[c] for c in both]
        if axis == "dy":
            rings = [ran(ring_turn(gate(own), *others)) for own, *others in sums]
    act, blocks = (), []
    for c in both:
        own, *others = sums[c]
        *act, block = ran(dense(c, (gate(own), *others), weight, bias_row, cotangent, act))
        blocks.append(block)

    gathered = lax.all_gather(blocks[0], "col", axis=0, tiled=True)
    joined = join((blocks[1],) + around(blocks[1], "dzh"))
    sources = (joined,) + around(joined, "dy")
    sources += tuple(send_col(source, dco=1) for source in sources)
    partial = backward(backs, numbers, (gathered,) + sources, tile_set)
    got = lax.all_to_all(partial.reshape(8, SENT, EDGE), "row", 0, 0, tiled=True)
    grad_features, grad_weight, grad_bias = last(got.reshape(8 * SENT, EDGE))
    return act[0], grad_features, grad_weight, grad_bias.reshape(EDGE)


def solution(mesh):
    placed = (
        P(("row", "col"), None),
        P("row", "col", None, None, None),
        P("row", "col", None),
        P("row", "col", None),
        P("row", "col"),
        P(),
        P(),
        P(("row", "col"), None),
    )
    return jax.shard_map(
        on_device,
        mesh=mesh,
        in_specs=placed,
        out_specs=(P(("row", "col"), None), P(("row", "col"), None), P(), P()),
        check_vma=False,
    )
```

profile of v0, /device:TPU:1, one launch (start us, length us, event | category | flops | bytes accessed | tf_op | source)
XLA Modules:
  0.0 255.0 jit_solution(3619220772298062103)
XLA Ops:
  15.1 3.4 %collective-permute-start.2 = (bf16[1024,128]{1,0:T(8,128)(2,1)}, bf16[1024,128]{1,0:T(8,128)(2,1)}, u32[]{:S(2)}, u32[]{:S(2)}) collective-permute-start(bf16[1024,128]{1,0:T(8,128)(2,1)} %collective-permute-done.1.refs_1_), channel_id=1, source_target_pairs={{0,192},{32,224},{64,0},{96,32},{128,64},{160,96},{192,128},{224,1... | collective-permute-start | bytes 786440 | tf_op jit(solution)/shard_map/ppermute | solution.py:50
  20.0 3.1 %collective-permute-done.2.refs_3_ = bf16[1024,128]{1,0:T(8,128)(2,1)} collective-permute-done((bf16[1024,128]{1,0:T(8,128)(2,1)}, bf16[1024,128]{1,0:T(8,128)(2,1)}, u32[]{:S(2)}, u32[]{:S(2)}) %collective-permute-start.2) | collective-permute-done | bytes 262176 | tf_op jit(solution)/shard_map/ppermute | solution.py:50
  23.1 3.4 %collective-permute-start.5 = (bf16[1024,128]{1,0:T(8,128)(2,1)}, bf16[1024,128]{1,0:T(8,128)(2,1)}, u32[]{:S(2)}, u32[]{:S(2)}) collective-permute-start(bf16[1024,128]{1,0:T(8,128)(2,1)} %collective-permute-done.2.refs_3_), channel_id=1, source_target_pairs={{0,192},{32,224},{64,0},{96,32},{128,64},{160,96},{192,128},{224,1... | collective-permute-start | bytes 786440 | tf_op jit(solution)/shard_map/ppermute | solution.py:50
  27.1 4.2 %bins.1 = (s32[1536]{0:T(1024)}, s32[8]{0:T(128)}) custom-call(s32[1,1]{1,0:T(1,128)S(6)} %copy.12.count_ref, s32[368]{0:T(512)} %get-tuple-element.110.part_ref, s32[368]{0:T(512)} %get-tuple-element.109.entry_ref), custom_call_target="tpu_custom_call" | custom-call | tf_op jit(solution)/shard_map/bins/pallas_call | solution.py:125
  34.3 7.3 %forward_send.2 = bf16[8192,128]{1,0:T(8,128)(2,1)} custom-call(s32[1536]{0:T(1024)} %get-tuple-element.61.list_ref, s32[8]{0:T(128)} %get-tuple-element.57.number_ref, bf16[1024,128]{1,0:T(8,128)(2,1)} %refs_0_.7, bf16[1024,128]{1,0:T(8,128)(2,1)} %collective-permute-done.1.refs_1_, bf16[1024,128]{1,0:T(8,128)(2,1)} %collective-permute-done.3.refs_2_, ...), custom_call_target="tpu_custom_call" | custom-call | tf_op jit(solution)/shard_map/forward_send/pallas_call | solution.py:276
  41.6 2.8 %collective-permute-start.7 = (bf16[8192,128]{1,0:T(8,128)(2,1)}, bf16[8192,128]{1,0:T(8,128)(2,1)}, u32[]{:S(2)}, u32[]{:S(2)}) collective-permute-start(bf16[8192,128]{1,0:T(8,128)(2,1)} %forward_send.2), channel_id=1, source_target_pairs={{0,1},{1,0},{2,3},{3,2},{4,5},{5,4},{6,7},{7,6},{8,9},{9,8},{10,11... | collective-permute-start | bytes 6291464 | tf_op jit(solution)/shard_map/ppermute | solution.py:54
  44.4 7.4 %forward_send.3 = bf16[8192,128]{1,0:T(8,128)(2,1)} custom-call(s32[1536]{0:T(1024)} %get-tuple-element.61.list_ref, s32[8]{0:T(128)} %get-tuple-element.57.number_ref, bf16[1024,128]{1,0:T(8,128)(2,1)} %refs_0_.7, bf16[1024,128]{1,0:T(8,128)(2,1)} %collective-permute-done.1.refs_1_, bf16[1024,128]{1,0:T(8,128)(2,1)} %collective-permute-done.3.refs_2_, ...), custom_call_target="tpu_custom_call" | custom-call | tf_op jit(solution)/shard_map/forward_send/pallas_call | solution.py:276
  51.9 8.0 %forward_keep.2 = (f32[2048,128]{1,0:T(8,128)}, bf16[2048,128]{1,0:T(8,128)(2,1)}, bf16[2048,128]{1,0:T(8,128)(2,1)}, f32[1024,128]{1,0:T(8,128)}, f32[1024,128]{1,0:T(8,128)}) custom-call(s32[1536]{0:T(1024)} %get-tuple-element.61.list_ref, s32[8]{0:T(128)} %get-tuple-element.57.number_ref, bf16[1024,128]{1,0:T(8,128)(2,1)} %refs_0_.7, ...), custom_call_target="tpu_custom_call" | custom-call | tf_op jit(solution)/shard_map/forward_keep/pallas_call | solution.py:288
  62.7 8.5 %forward_keep.3 = (f32[2048,128]{1,0:T(8,128)}, bf16[2048,128]{1,0:T(8,128)(2,1)}, bf16[2048,128]{1,0:T(8,128)(2,1)}, f32[1024,128]{1,0:T(8,128)}, f32[1024,128]{1,0:T(8,128)}) custom-call(s32[1536]{0:T(1024)} %get-tuple-element.61.list_ref, s32[8]{0:T(128)} %get-tuple-element.57.number_ref, bf16[1024,128]{1,0:T(8,128)(2,1)} %refs_0_.7, ...), custom_call_target="tpu_custom_call" | custom-call | tf_op jit(solution)/shard_map/forward_keep/pallas_call | solution.py:288
  78.8 6.7 %collective-permute-done.11.from_left.refs_1_ = bf16[2048,128]{1,0:T(8,128)(2,1)} collective-permute-done((bf16[2048,128]{1,0:T(8,128)(2,1)}, bf16[2048,128]{1,0:T(8,128)(2,1)}, u32[]{:S(2)}, u32[]{:S(2)}) %collective-permute-start.11) | collective-permute-done | bytes 524320 | tf_op jit(solution)/shard_map/ppermute | solution.py:54
  94.1 6.0 %collective-permute-start.18 = (bf16[512,128]{1,0:T(8,128)(2,1)}, bf16[512,128]{1,0:T(8,128)(2,1)}, u32[]{:S(2)}, u32[]{:S(2)}) collective-permute-start(bf16[512,128]{1,0:T(8,128)(2,1)} %get-tuple-element.86), channel_id=1, source_target_pairs={{0,6},{1,7},{2,0},{3,1},{4,2},{5,3},{6,4},{7,5},{8,14},{9,15},{10,... | collective-permute-start | bytes 393224 | tf_op jit(solution)/shard_map/ppermute | solution.py:54
  103.1 5.5 %collective-permute-start.20 = (bf16[512,128]{1,0:T(8,128)(2,1)}, bf16[512,128]{1,0:T(8,128)(2,1)}, u32[]{:S(2)}, u32[]{:S(2)}) collective-permute-start(bf16[512,128]{1,0:T(8,128)(2,1)} %get-tuple-element.91), channel_id=1, source_target_pairs={{0,6},{1,7},{2,0},{3,1},{4,2},{5,3},{6,4},{7,5},{8,14},{9,15},{10,... | collective-permute-start | bytes 393224 | tf_op jit(solution)/shard_map/ppermute | solution.py:54
  125.0 2.8 %collective-permute-done.23.refs_3_ = bf16[256,128]{1,0:T(8,128)(2,1)} collective-permute-done((bf16[256,128]{1,0:T(8,128)(2,1)}, bf16[256,128]{1,0:T(8,128)(2,1)}, u32[]{:S(2)}, u32[]{:S(2)}) %collective-permute-start.23) | collective-permute-done | bytes 65568 | tf_op jit(solution)/shard_map/ppermute | solution.py:54
  130.2 3.6 %collective-permute-start.25 = (bf16[672,128]{1,0:T(8,128)(2,1)}, bf16[672,128]{1,0:T(8,128)(2,1)S(1)}, u32[]{:S(2)}, u32[]{:S(2)}) collective-permute-start(bf16[672,128]{1,0:T(8,128)(2,1)} %get-tuple-element.100.refs_0_), channel_id=1, source_target_pairs={{0,6},{1,7},{2,0},{3,1},{4,2},{5,3},{6,4},{7,5},{8,14},{9,15},{10,... | collective-permute-start | bytes 516104 | tf_op jit(solution)/shard_map/ppermute | solution.py:54
  133.8 4.3 %collective-permute-done.26.refs_4_ = bf16[672,128]{1,0:T(8,128)(2,1)S(1)} collective-permute-done((bf16[672,128]{1,0:T(8,128)(2,1)}, bf16[672,128]{1,0:T(8,128)(2,1)S(1)}, u32[]{:S(2)}, u32[]{:S(2)}) %collective-permute-start.26) | collective-permute-done | bytes 172064 | tf_op jit(solution)/shard_map/ppermute | solution.py:54
  141.9 4.4 %collective-permute-start.28 = (bf16[336,128]{1,0:T(8,128)(2,1)S(1)}, bf16[336,128]{1,0:T(8,128)(2,1)}, u32[]{:S(2)}, u32[]{:S(2)}) collective-permute-start(bf16[336,128]{1,0:T(8,128)(2,1)S(1)} %slice.17), channel_id=1, source_target_pairs={{0,6},{1,7},{2,0},{3,1},{4,2},{5,3},{6,4},{7,5},{8,14},{9,15},{10,... | collective-permute-start | bytes 258056 | tf_op jit(solution)/shard_map/ppermute | solution.py:54
  150.8 2.7 %collective-permute-start.29 = (bf16[2688,128]{1,0:T(8,128)(2,1)}, bf16[2688,128]{1,0:T(8,128)(2,1)S(1)}, u32[]{:S(2)}, u32[]{:S(2)}) collective-permute-start(bf16[2688,128]{1,0:T(8,128)(2,1)} %join.1.refs_1_), channel_id=1, source_target_pairs={{0,24},{1,25},{2,26},{3,27},{4,28},{5,29},{6,30},{7,31},{8,0},{9,1... | collective-permute-start | bytes 2064392 | tf_op jit(solution)/shard_map/ppermute | solution.py:54
  153.5 8.4 %collective-permute-start.33 = (bf16[2688,128]{1,0:T(8,128)(2,1)}, bf16[2688,128]{1,0:T(8,128)(2,1)S(1)}, u32[]{:S(2)}, u32[]{:S(2)}) collective-permute-start(bf16[2688,128]{1,0:T(8,128)(2,1)} %join.1.refs_1_), channel_id=1, source_target_pairs={{0,1},{1,0},{2,3},{3,2},{4,5},{5,4},{6,7},{7,6},{8,9},{9,8},{10,11... | collective-permute-start | bytes 2064392 | tf_op jit(solution)/shard_map/ppermute | solution.py:54
  162.2 2.7 %collective-permute-start.32 = (bf16[1344,128]{1,0:T(8,128)(2,1)S(1)}, bf16[1344,128]{1,0:T(8,128)(2,1)S(1)}, u32[]{:S(2)}, u32[]{:S(2)}) collective-permute-start(bf16[1344,128]{1,0:T(8,128)(2,1)S(1)} %slice.19), channel_id=1, source_target_pairs={{0,24},{1,25},{2,26},{3,27},{4,28},{5,29},{6,30},{7,31},{8,0},{9,1... | collective-permute-start | bytes 1032200 | tf_op jit(solution)/shard_map/ppermute | solution.py:54
  164.9 22.2 %collective-permute-start.37 = (bf16[2688,128]{1,0:T(8,128)(2,1)S(1)}, bf16[2688,128]{1,0:T(8,128)(2,1)S(1)}, u32[]{:S(2)}, u32[]{:S(2)}) collective-permute-start(bf16[2688,128]{1,0:T(8,128)(2,1)S(1)} %collective-permute-done.30.refs_5_), channel_id=1, source_target_pairs={{0,1},{1,0},{2,3},{3,2},{4,5},{5,4},{6,7},{7,6},{8,9},{9,8},{10,11... | collective-permute-start | bytes 2064392 | tf_op jit(solution)/shard_map/ppermute | solution.py:54
  187.1 4.8 %collective-permute-start.35 = (bf16[1344,128]{1,0:T(8,128)(2,1)S(1)}, bf16[1344,128]{1,0:T(8,128)(2,1)S(1)}, u32[]{:S(2)}, u32[]{:S(2)}) collective-permute-start(bf16[1344,128]{1,0:T(8,128)(2,1)S(1)} %collective-permute-done.31.refs_3_), channel_id=1, source_target_pairs={{0,1},{1,0},{2,3},{3,2},{4,5},{5,4},{6,7},{7,6},{8,9},{9,8},{10,11... | collective-permute-start | bytes 1032200 | tf_op jit(solution)/shard_map/ppermute | solution.py:54
  194.9 18.1 %backward.1 = bf16[9344,128]{1,0:T(8,128)(2,1)} custom-call(s32[368]{0:T(512)} %get-tuple-element.108.back_ref, s32[8]{0:T(128)} %get-tuple-element.57.number_ref, bf16[20992,128]{1,0:T(8,128)(2,1)} %all-gather.2.cloned.1.call-done.refs_0_, bf16[2688,128]{1,0:T(8,128)(2,1)} %join.1.refs_1_, bf16[2688,128]{1,0:T(8,128)(2,1)} %copy-done.1, ...), custom_call_target="tpu_custom_call" | custom-call | tf_op jit(solution)/shard_map/backward/pallas_call | solution.py:494
  213.1 32.3 %all_to_all.5 = bf16[8,1168,128]{2,1,0:T(8,128)(2,1)} all-to-all(bf16[8,1168,128]{2,1,0:T(8,128)(2,1)} %bitcast.10), channel_id=1, replica_groups=mesh['row'=8,'col'=32] {'row'}, dimensions={0} | all-to-all | bytes 4784128 | tf_op jit(solution)/shard_map/all_to_all | solution.py:596
  245.4 2.7 %last.1 = (bf16[1024,128]{1,0:T(8,128)(2,1)}, f32[128,128]{1,0:T(8,128)}, f32[1,128]{1,0:T(1,128)}) custom-call(bf16[9344,128]{1,0:T(8,128)(2,1)} %bitcast.11), custom_call_target="tpu_custom_call" | custom-call | tf_op jit(solution)/shard_map/last/pallas_call | solution.py:525
  (101 shorter events, 64.9 us)
Async XLA Ops:
  7.2 187.8 %all-gather.2.cloned.1.call-start = ((), (), s32[]{:S(2)}) async-start(), calls=%async_computation.1 | async-start | bytes 5541888 | tf_op jit(solution)/shard_map/all_gather | solution.py:591
  18.5 12.8 %collective-permute-start.3 = (bf16[1024,128]{1,0:T(8,128)(2,1)}, bf16[1024,128]{1,0:T(8,128)(2,1)}, u32[]{:S(2)}, u32[]{:S(2)}) collective-permute-start(bf16[1024,128]{1,0:T(8,128)(2,1)} %refs_0_.7), channel_id=1, source_target_pairs={{0,192},{32,224},{64,0},{96,32},{128,64},{160,96},{192,128},{224,1... | collective-permute-start | bytes 786440 | tf_op jit(solution)/shard_map/ppermute | solution.py:50
  19.0 12.3 %collective-permute-start.6 = (bf16[1024,128]{1,0:T(8,128)(2,1)}, bf16[1024,128]{1,0:T(8,128)(2,1)}, u32[]{:S(2)}, u32[]{:S(2)}) collective-permute-start(bf16[1024,128]{1,0:T(8,128)(2,1)} %collective-permute-done.1.refs_1_), channel_id=1, source_target_pairs={{0,64},{32,96},{64,128},{96,160},{128,192},{160,224},{192,0},{224,... | collective-permute-start | bytes 786440 | tf_op jit(solution)/shard_map/ppermute | solution.py:50
  19.9 12.1 %collective-permute-start.4 = (bf16[1024,128]{1,0:T(8,128)(2,1)}, bf16[1024,128]{1,0:T(8,128)(2,1)}, u32[]{:S(2)}, u32[]{:S(2)}) collective-permute-start(bf16[1024,128]{1,0:T(8,128)(2,1)} %collective-permute-done.refs_6_), channel_id=1, source_target_pairs={{0,64},{32,96},{64,128},{96,160},{128,192},{160,224},{192,0},{224,... | collective-permute-start | bytes 786440 | tf_op jit(solution)/shard_map/ppermute | solution.py:50
  23.1 11.2 %collective-permute-start.5 = (bf16[1024,128]{1,0:T(8,128)(2,1)}, bf16[1024,128]{1,0:T(8,128)(2,1)}, u32[]{:S(2)}, u32[]{:S(2)}) collective-permute-start(bf16[1024,128]{1,0:T(8,128)(2,1)} %collective-permute-done.2.refs_3_), channel_id=1, source_target_pairs={{0,192},{32,224},{64,0},{96,32},{128,64},{160,96},{192,128},{224,1... | collective-permute-start | bytes 786440 | tf_op jit(solution)/shard_map/ppermute | solution.py:50
  51.8 10.8 %collective-permute-start.8 = (bf16[8192,128]{1,0:T(8,128)(2,1)}, bf16[8192,128]{1,0:T(8,128)(2,1)}, u32[]{:S(2)}, u32[]{:S(2)}) collective-permute-start(bf16[8192,128]{1,0:T(8,128)(2,1)} %forward_send.3), channel_id=1, source_target_pairs={{0,1},{1,0},{2,3},{3,2},{4,5},{5,4},{6,7},{7,6},{8,9},{9,8},{10,11... | collective-permute-start | bytes 6291464 | tf_op jit(solution)/shard_map/ppermute | solution.py:54
  59.9 14.1 %collective-permute-start.9 = (bf16[2048,128]{1,0:T(8,128)(2,1)}, bf16[2048,128]{1,0:T(8,128)(2,1)}, u32[]{:S(2)}, u32[]{:S(2)}) collective-permute-start(bf16[2048,128]{1,0:T(8,128)(2,1)} %get-tuple-element.67), channel_id=1, source_target_pairs={{0,8},{1,9},{2,10},{3,11},{4,12},{5,13},{6,14},{7,15},{8,16},{9,17... | collective-permute-start | bytes 1572872 | tf_op jit(solution)/shard_map/ppermute | solution.py:54
  60.0 14.0 %collective-permute-start.10 = (bf16[2048,128]{1,0:T(8,128)(2,1)}, bf16[2048,128]{1,0:T(8,128)(2,1)}, u32[]{:S(2)}, u32[]{:S(2)}) collective-permute-start(bf16[2048,128]{1,0:T(8,128)(2,1)} %get-tuple-element.68), channel_id=1, source_target_pairs={{0,24},{1,25},{2,26},{3,27},{4,28},{5,29},{6,30},{7,31},{8,0},{9,1... | collective-permute-start | bytes 1572872 | tf_op jit(solution)/shard_map/ppermute | solution.py:54
  71.2 14.2 %collective-permute-start.11 = (bf16[2048,128]{1,0:T(8,128)(2,1)}, bf16[2048,128]{1,0:T(8,128)(2,1)}, u32[]{:S(2)}, u32[]{:S(2)}) collective-permute-start(bf16[2048,128]{1,0:T(8,128)(2,1)} %get-tuple-element.72), channel_id=1, source_target_pairs={{0,8},{1,9},{2,10},{3,11},{4,12},{5,13},{6,14},{7,15},{8,16},{9,17... | collective-permute-start | bytes 1572872 | tf_op jit(solution)/shard_map/ppermute | solution.py:54
  71.3 14.2 %collective-permute-start.12 = (bf16[2048,128]{1,0:T(8,128)(2,1)}, bf16[2048,128]{1,0:T(8,128)(2,1)}, u32[]{:S(2)}, u32[]{:S(2)}) collective-permute-start(bf16[2048,128]{1,0:T(8,128)(2,1)} %get-tuple-element.73), channel_id=1, source_target_pairs={{0,24},{1,25},{2,26},{3,27},{4,28},{5,29},{6,30},{7,31},{8,0},{9,1... | collective-permute-start | bytes 1572872 | tf_op jit(solution)/shard_map/ppermute | solution.py:54
  76.4 13.8 %collective-permute-start.14 = (bf16[1024,128]{1,0:T(8,128)(2,1)}, bf16[1024,128]{1,0:T(8,128)(2,1)}, u32[]{:S(2)}, u32[]{:S(2)}) collective-permute-start(bf16[1024,128]{1,0:T(8,128)(2,1)} %get-tuple-element.76), channel_id=1, source_target_pairs={{0,24},{1,25},{2,26},{3,27},{4,28},{5,29},{6,30},{7,31},{8,0},{9,1... | collective-permute-start | bytes 786440 | tf_op jit(solution)/shard_map/ppermute | solution.py:54
  78.8 12.3 %collective-permute-start.13 = (bf16[1024,128]{1,0:T(8,128)(2,1)}, bf16[1024,128]{1,0:T(8,128)(2,1)}, u32[]{:S(2)}, u32[]{:S(2)}) collective-permute-start(bf16[1024,128]{1,0:T(8,128)(2,1)} %get-tuple-element.69), channel_id=1, source_target_pairs={{0,8},{1,9},{2,10},{3,11},{4,12},{5,13},{6,14},{7,15},{8,16},{9,17... | collective-permute-start | bytes 786440 | tf_op jit(solution)/shard_map/ppermute | solution.py:54
  87.8 12.3 %collective-permute-start.16 = (bf16[1024,128]{1,0:T(8,128)(2,1)}, bf16[1024,128]{1,0:T(8,128)(2,1)}, u32[]{:S(2)}, u32[]{:S(2)}) collective-permute-start(bf16[1024,128]{1,0:T(8,128)(2,1)} %get-tuple-element.79), channel_id=1, source_target_pairs={{0,24},{1,25},{2,26},{3,27},{4,28},{5,29},{6,30},{7,31},{8,0},{9,1... | collective-permute-start | bytes 786440 | tf_op jit(solution)/shard_map/ppermute | solution.py:54
  93.7 14.9 %collective-permute-start.17 = (bf16[512,128]{1,0:T(8,128)(2,1)}, bf16[512,128]{1,0:T(8,128)(2,1)}, u32[]{:S(2)}, u32[]{:S(2)}) collective-permute-start(bf16[512,128]{1,0:T(8,128)(2,1)} %get-tuple-element.85), channel_id=1, source_target_pairs={{0,2},{1,3},{2,4},{3,5},{4,6},{5,7},{6,0},{7,1},{8,10},{9,11},{10,... | collective-permute-start | bytes 393224 | tf_op jit(solution)/shard_map/ppermute | solution.py:54
  94.1 14.4 %collective-permute-start.18 = (bf16[512,128]{1,0:T(8,128)(2,1)}, bf16[512,128]{1,0:T(8,128)(2,1)}, u32[]{:S(2)}, u32[]{:S(2)}) collective-permute-start(bf16[512,128]{1,0:T(8,128)(2,1)} %get-tuple-element.86), channel_id=1, source_target_pairs={{0,6},{1,7},{2,0},{3,1},{4,2},{5,3},{6,4},{7,5},{8,14},{9,15},{10,... | collective-permute-start | bytes 393224 | tf_op jit(solution)/shard_map/ppermute | solution.py:54
  102.7 12.6 %collective-permute-start.19 = (bf16[512,128]{1,0:T(8,128)(2,1)}, bf16[512,128]{1,0:T(8,128)(2,1)}, u32[]{:S(2)}, u32[]{:S(2)}) collective-permute-start(bf16[512,128]{1,0:T(8,128)(2,1)} %get-tuple-element.90), channel_id=1, source_target_pairs={{0,2},{1,3},{2,4},{3,5},{4,6},{5,7},{6,0},{7,1},{8,10},{9,11},{10,... | collective-permute-start | bytes 393224 | tf_op jit(solution)/shard_map/ppermute | solution.py:54
  103.1 12.2 %collective-permute-start.20 = (bf16[512,128]{1,0:T(8,128)(2,1)}, bf16[512,128]{1,0:T(8,128)(2,1)}, u32[]{:S(2)}, u32[]{:S(2)}) collective-permute-start(bf16[512,128]{1,0:T(8,128)(2,1)} %get-tuple-element.91), channel_id=1, source_target_pairs={{0,6},{1,7},{2,0},{3,1},{4,2},{5,3},{6,4},{7,5},{8,14},{9,15},{10,... | collective-permute-start | bytes 393224 | tf_op jit(solution)/shard_map/ppermute | solution.py:54
  130.2 11.0 %collective-permute-start.25 = (bf16[672,128]{1,0:T(8,128)(2,1)}, bf16[672,128]{1,0:T(8,128)(2,1)S(1)}, u32[]{:S(2)}, u32[]{:S(2)}) collective-permute-start(bf16[672,128]{1,0:T(8,128)(2,1)} %get-tuple-element.100.refs_0_), channel_id=1, source_target_pairs={{0,6},{1,7},{2,0},{3,1},{4,2},{5,3},{6,4},{7,5},{8,14},{9,15},{10,... | collective-permute-start | bytes 516104 | tf_op jit(solution)/shard_map/ppermute | solution.py:54
  150.8 11.2 %collective-permute-start.30 = (bf16[2688,128]{1,0:T(8,128)(2,1)}, bf16[2688,128]{1,0:T(8,128)(2,1)S(1)}, u32[]{:S(2)}, u32[]{:S(2)}) collective-permute-start(bf16[2688,128]{1,0:T(8,128)(2,1)} %join.1.refs_1_), channel_id=1, source_target_pairs={{0,8},{1,9},{2,10},{3,11},{4,12},{5,13},{6,14},{7,15},{8,16},{9,17... | collective-permute-start | bytes 2064392 | tf_op jit(solution)/shard_map/ppermute | solution.py:54
  150.8 11.3 %collective-permute-start.29 = (bf16[2688,128]{1,0:T(8,128)(2,1)}, bf16[2688,128]{1,0:T(8,128)(2,1)S(1)}, u32[]{:S(2)}, u32[]{:S(2)}) collective-permute-start(bf16[2688,128]{1,0:T(8,128)(2,1)} %join.1.refs_1_), channel_id=1, source_target_pairs={{0,24},{1,25},{2,26},{3,27},{4,28},{5,29},{6,30},{7,31},{8,0},{9,1... | collective-permute-start | bytes 2064392 | tf_op jit(solution)/shard_map/ppermute | solution.py:54
  153.5 38.6 %collective-permute-start.33 = (bf16[2688,128]{1,0:T(8,128)(2,1)}, bf16[2688,128]{1,0:T(8,128)(2,1)S(1)}, u32[]{:S(2)}, u32[]{:S(2)}) collective-permute-start(bf16[2688,128]{1,0:T(8,128)(2,1)} %join.1.refs_1_), channel_id=1, source_target_pairs={{0,1},{1,0},{2,3},{3,2},{4,5},{5,4},{6,7},{7,6},{8,9},{9,8},{10,11... | collective-permute-start | bytes 2064392 | tf_op jit(solution)/shard_map/ppermute | solution.py:54
  162.0 25.1 %collective-permute-start.31 = (bf16[1344,128]{1,0:T(8,128)(2,1)S(1)}, bf16[1344,128]{1,0:T(8,128)(2,1)S(1)}, u32[]{:S(2)}, u32[]{:S(2)}) collective-permute-start(bf16[1344,128]{1,0:T(8,128)(2,1)S(1)} %slice.18), channel_id=1, source_target_pairs={{0,8},{1,9},{2,10},{3,11},{4,12},{5,13},{6,14},{7,15},{8,16},{9,17... | collective-permute-start | bytes 1032200 | tf_op jit(solution)/shard_map/ppermute | solution.py:54
  162.2 29.8 %collective-permute-start.32 = (bf16[1344,128]{1,0:T(8,128)(2,1)S(1)}, bf16[1344,128]{1,0:T(8,128)(2,1)S(1)}, u32[]{:S(2)}, u32[]{:S(2)}) collective-permute-start(bf16[1344,128]{1,0:T(8,128)(2,1)S(1)} %slice.19), channel_id=1, source_target_pairs={{0,24},{1,25},{2,26},{3,27},{4,28},{5,29},{6,30},{7,31},{8,0},{9,1... | collective-permute-start | bytes 1032200 | tf_op jit(solution)/shard_map/ppermute | solution.py:54
  164.9 28.3 %collective-permute-start.37 = (bf16[2688,128]{1,0:T(8,128)(2,1)S(1)}, bf16[2688,128]{1,0:T(8,128)(2,1)S(1)}, u32[]{:S(2)}, u32[]{:S(2)}) collective-permute-start(bf16[2688,128]{1,0:T(8,128)(2,1)S(1)} %collective-permute-done.30.refs_5_), channel_id=1, source_target_pairs={{0,1},{1,0},{2,3},{3,2},{4,5},{5,4},{6,7},{7,6},{8,9},{9,8},{10,11... | collective-permute-start | bytes 2064392 | tf_op jit(solution)/shard_map/ppermute | solution.py:54
  (26 other events, 156.7 us)
Sparse Core Ops, SparseCore 0:
  120.7 69.8 all-gather.1
where the time goes:
time: 260 us; the launch traced here: 255 us
  starting transfers between devices  91.4 us (35%)
  Pallas kernels  76.6 us (29%)
  waiting for transfers between devices  34.5 us (13%)
  blocking collectives  32.3 us (12%)
  between operations  14.9 us (6%)
  local copies, waits for them, and re-layouts  3.28 us (1%)
    ppermute x31, starting transfers between devices, send_col(): return lax.ppermute(value, 'col', col_perm(**step))  79.2 us
    all_to_all x1, blocking collectives, on_device(): lax.all_to_all(partial.reshape(8, SENT, EDGE), 'row', 0, 0, tiled=True)  32.3 us
    ppermute x31, waiting for transfers between devices, send_col(): return lax.ppermute(value, 'col', col_perm(**step))  26.4 us
    pallas_call x1, Pallas kernels, backward(): pl.pallas_call(functools.partial(backward_kernel, sizes), out_shape=shape...  18.1 us
    pallas_call x2, Pallas kernels, forward_keep(): pl.pallas_call(functools.partial(forward_keep_kernel, part), out_shape=re...  16.5 us
    pallas_call x2, Pallas kernels, forward_send(): pl.pallas_call(functools.partial(forward_send_kernel, part), out_shape=sh...  14.7 us
    ppermute x7, starting transfers between devices, send_row(): return lax.ppermute(value, 'row', row_perm(**step))  12.1 us
    pallas_call x4, Pallas kernels, relay_middle(): pl.pallas_call(middle_kernel, out_shape=(shape_of(rest_right.shape[0], BF...  8.24 us
  transfers between devices with their start and end apart: 39, of which 17 were waited for; matrix products, arithmetic and copies ran while one was open for 1% of the time, Pallas kernels for 18%

commit v1 on v0

--- a/solution.py
+++ b/solution.py
@@ -12,8 +12,7 @@
 PARTS = (4, 4)
 AREAS = tuple(NY * NZH * tiles for tiles in PARTS)
 TERMS = EDGE + 16
-BLOCK0 = PARTS[0] * EDGE + TERMS
-BLOCK1 = PARTS[1] * EDGE + TERMS + 16
+BLOCK = PARTS[1] * EDGE + TERMS
 SENT = 8 * EDGE + TERMS
 GROUP = 8
 SLOTS = 384
@@ -88,10 +87,8 @@
     row_place = jnp.where(later, ring * PARTS[1] + inner - PARTS[0], ring * PARTS[0] + inner)
     source = jnp.where(
         later,
-        (NY * NZH * NCO * BLOCK0 + TERMS + 16) // 16
-        + (other * NY * NZH + ring) * (BLOCK1 // 16)
-        + (inner - PARTS[0]) * (EDGE // 16),
-        owner * (BLOCK0 // 16) + inner * (EDGE // 16),
+        owner * (BLOCK // 16) + (inner - PARTS[0]) * (EDGE // 16),
+        (other * AREAS[0] + row_place) * (EDGE // 16),
     )
     backward = col_tiles | (source << 7)
     owner, inner = col_tiles >> 3, col_tiles & 7
@@ -101,7 +98,7 @@
     return part, slot | (col_place << 9) | (row_place << 16), backward
 
 
-def bins_kernel(count_ref, part_ref, entry_ref, list_ref, number_ref):
+def bins_kernel(count_ref, part_ref, entry_ref, back_ref, list_ref, backs_ref, number_ref):
     for part in range(4):
         number_ref[part] = 0
 
@@ -109,30 +106,31 @@
         part = part_ref[slot]
         at = number_ref[part]
         list_ref[part * SLOTS + at] = entry_ref[slot]
+        backs_ref[part * SLOTS + at] = back_ref[slot]
         number_ref[part] = at + 1
         return carry
 
-    count = count_ref[0, 0]
-    number_ref[4] = count
-    lax.fori_loop(0, count, one, 0)
+    lax.fori_loop(0, count_ref[0, 0], one, 0)
     for part in range(4):
         last = number_ref[part]
         for extra in range(GROUP - 1):
             list_ref[part * SLOTS + last + extra] = 64 << 9
-
-
-def make_bins(count, part, entry):
+            backs_ref[part * SLOTS + last + extra] = 64
+
+
+def make_bins(count, part, entry, back):
     return pl.pallas_call(
         bins_kernel,
         out_shape=(
             jax.ShapeDtypeStruct((4 * SLOTS,), jnp.int32),
-            jax.ShapeDtypeStruct((8,), jnp.int32),
+            jax.ShapeDtypeStruct((4 * SLOTS,), jnp.int32),
+            jax.ShapeDtypeStruct((4,), jnp.int32),
         ),
-        in_specs=[in_smem()] * 3,
-        out_specs=(in_smem(),) * 2,
+        in_specs=[in_smem()] * 4,
+        out_specs=(in_smem(),) * 3,
         compiler_params=params(),
         name="bins",
-    )(count, part, entry)
+    )(count, part, entry, back)
 
 
 def groups_of(number_ref, part):
@@ -257,6 +255,17 @@
         rest_left[at, :] = read(3 * block + half + k, 64)
 
 
+def split_direct(read, own, first, second, third):
+    block = own.shape[0]
+    for n, target in enumerate((own, first, second, third)):
+        for k in range(0, block, 64):
+            target[pl.ds(k, 64), :] = read(n * block + k, 64).astype(target.dtype)
+
+
+def direct_shapes(block):
+    return (shape_of(block, F32),) + (shape_of(block, BF),) * 3
+
+
 def relay_shapes(block):
     half = block // 2
     return (shape_of(block, F32),) + (shape_of(block, BF),) * 2 + (shape_of(half, F32),) * 2
@@ -296,6 +305,17 @@
     )(lists, numbers, *pieces, tiles, got)
 
 
+def direct_total(own, got):
+    def read(k, rows):
+        at = pl.ds(k, rows)
+        total = own[at, :]
+        for piece in got:
+            total += piece[at, :].astype(F32)
+        return total
+
+    return read
+
+
 def relay_total(own, from_left, from_right, late_left, late_right):
     half = late_left.shape[0]
 
@@ -326,15 +346,15 @@
 
 
 def turn_kernel(*refs):
-    split_relay(relay_total(*refs[:5]), *refs[5:])
+    split_direct(relay_total(*refs[:5]), *refs[5:])
 
 
 def ring_turn(*values):
     return pl.pallas_call(
         turn_kernel,
-        out_shape=relay_shapes(values[0].shape[0] // 4),
+        out_shape=direct_shapes(values[0].shape[0] // 4),
         in_specs=[in_vmem()] * 5,
-        out_specs=(in_vmem(),) * 5,
+        out_specs=(in_vmem(),) * 4,
         compiler_params=params(),
         name="turn",
     )(*values)
@@ -360,152 +380,133 @@
 
 
 def dense_kernel(chunk, *refs):
-    sums, (weight_ref, bias_ref, cot_ref), outs = refs[:5], refs[5:8], refs[8:]
+    sums, (weight_ref, bias_ref, cot_ref), outs = refs[:4], refs[4:7], refs[7:]
     rows = PARTS[chunk] * EDGE
     skip = chunk * PARTS[0] * EDGE
-    read = relay_total(*sums)
-    hidden = jnp.concatenate([read(k, rows // 2).astype(BF) for k in (0, rows // 2)], axis=0)
+    hidden = direct_total(sums[0], sums[1:])(0, rows).astype(BF)
     weight = weight_ref[...]
     pre = jnp.dot(hidden, weight, preferred_element_type=F32) + bias_ref[...]
     sigma = jax.nn.sigmoid(pre)
     act = (pre * sigma).astype(BF)
-    if chunk:
-        act_in, (act_ref, block_ref) = outs[0], outs[1:]
-        act_ref[pl.ds(0, skip), :] = act_in[...]
-        act_ref[pl.ds(skip, rows), :] = act
-        terms_at, back_at = 0, TERMS + 16
-        block_ref[pl.ds(TERMS, 16), :] = jnp.zeros((16, EDGE), BF)
-    else:
-        act_ref, block_ref = outs
-        act_ref[...] = act
-        terms_at, back_at = rows, 0
     grad_pre = cot_ref[pl.ds(skip, rows), :].astype(F32) * sigma * (1.0 + pre * (1.0 - sigma))
     grad_round = grad_pre.astype(BF)
     weight_term = lax.dot_general(hidden, grad_round, (((0,), (0,)), ((), ())), preferred_element_type=F32)
     bias_term = jnp.broadcast_to(jnp.sum(grad_pre, axis=0, keepdims=True), (16, EDGE))
-    block_ref[pl.ds(terms_at, EDGE), :] = weight_term.astype(BF)
-    block_ref[pl.ds(terms_at + EDGE, 16), :] = bias_term.astype(BF)
+    if chunk:
+        act_in, terms_in, act_ref, block_ref = outs
+        act_ref[pl.ds(0, skip), :] = act_in[...]
+        act_ref[pl.ds(skip, rows), :] = act
+        block_ref[pl.ds(rows, EDGE), :] = (terms_in[pl.ds(0, EDGE), :] + weight_term).astype(BF)
+        block_ref[pl.ds(rows + EDGE, 16), :] = (terms_in[pl.ds(EDGE, 16), :] + bias_term).astype(BF)
+    else:
+        act_ref, block_ref, terms_ref = outs
+        act_ref[...] = act
+        terms_ref[pl.ds(0, EDGE), :] = weight_term
+        terms_ref[pl.ds(EDGE, 16), :] = bias_term
     for tile in range(PARTS[chunk]):
         part = grad_round[tile * EDGE : (tile + 1) * EDGE, :]
         back = lax.dot_general(weight, part, (((1,), (1,)), ((), ())), preferred_element_type=F32)
-        block_ref[pl.ds(back_at + tile * EDGE, EDGE), :] = back.astype(BF)
+        block_ref[pl.ds(tile * EDGE, EDGE), :] = back.astype(BF)
 
 
 def dense(chunk, sums, weight, bias, cotangent, before):
+    rows = PARTS[chunk] * EDGE
+    outs = (shape_of(sum(PARTS[: chunk + 1]) * EDGE, BF),)
+    outs += (shape_of(BLOCK, BF),) if chunk else (shape_of(rows, BF), shape_of(TERMS, F32))
     return pl.pallas_call(
         functools.partial(dense_kernel, chunk),
-        out_shape=(
-            shape_of(sum(PARTS[: chunk + 1]) * EDGE, BF),
-            shape_of((BLOCK0, BLOCK1)[chunk], BF),
-        ),
-        in_specs=[in_vmem()] * (8 + len(before)),
-        out_specs=(in_vmem(),) * 2,
+        out_shape=outs,
+        in_specs=[in_vmem()] * (7 + len(before)),
+        out_specs=(in_vmem(),) * len(outs),
         compiler_params=params(),
         name="dense",
     )(*sums, weight, bias, cotangent, *before)
 
 
-def both_ways(values):
-    return (values[0] + values[2]) + (values[1] + values[3])
-
-
-def backward_kernel(sizes, back_ref, number_ref, *refs):
+def backward_kernel(chunk, sizes, list_ref, backs_ref, number_ref, *refs):
     count = len(sizes)
     sources, tiles_ref = refs[:count], refs[count]
-    out_ref, gbuf, tbuf, acc, gsem, tsem = refs[count + 1 :]
-    groups = (number_ref[4] + (GROUP - 1)) // GROUP
-    slots = tiles_ref.shape[0]
+    out_ref, gbuf, tbuf, acc, gsem, tsem, bsem = refs[-7:]
+    parts = (2 * chunk, 2 * chunk + 1)
+    groups = [groups_of(number_ref, part) for part in parts]
     copies, at = [], 0
     for k, size in enumerate(sizes):
         copies.append(pltpu.make_async_copy(sources[k], gbuf.at[pl.ds(at, size)], gsem.at[k]))
         at += size
+    if chunk:
+        copies.append(pltpu.make_async_copy(refs[count + 1], acc.at[pl.ds(0, 64 * EDGE)], bsem.at[0]))
     for copy in copies:
         copy.start()
-
-    def tile_copy(group):
-        at = pl.ds(group * GROUP, GROUP)
-        return pltpu.make_async_copy(tiles_ref.at[at], tbuf.at[at], tsem.at[group])
-
-    def issue(group, carry):
-        tile_copy(group).start()
-        return carry
-
-    lax.fori_loop(0, groups, issue, 0)
+    start_tiles(list_ref, tiles_ref, tbuf, tsem, parts[0], groups[0], 0)
+    start_tiles(list_ref, tiles_ref, tbuf, tsem, parts[1], groups[1], groups[0])
 
     def clear(at):
         acc[at, :] = jnp.zeros((EDGE, EDGE), F32)
 
-    over_tiles(65, clear)
+    if chunk:
+        clear(pl.ds(64 * EDGE, EDGE))
+    else:
+        over_tiles(65, clear)
     for copy in copies:
         copy.wait()
-
-    def entry_of(slot):
-        return jnp.where(slot < number_ref[4], back_ref[jnp.minimum(slot, slots - 1)], 64)
-
-    def body(group, carry):
-        tile_copy(group).wait()
-        for first in range(0, GROUP, BATCH):
-            entries = [entry_of(group * GROUP + first + k) for k in range(BATCH)]
-            products = [
-                jnp.dot(
-                    gbuf[pl.ds(pl.multiple_of((entry >> 7) * 16, 16), EDGE), :],
-                    tbuf[group * GROUP + first + k],
-                    preferred_element_type=F32,
-                )
-                for k, entry in enumerate(entries)
-            ]
-            for entry, product in zip(entries, products):
-                acc[place(entry & 127), :] += product
-        return carry
-
-    lax.fori_loop(0, groups, body, 0)
-
-    second = NY * NZH * NCO * BLOCK0
-
-    def terms_of(k, rows):
-        total = jnp.zeros((rows, EDGE), F32)
+    for which, part in enumerate(parts):
+        first_group = groups[0] * which
+
+        def body(group, carry):
+            wait_group(tiles_ref, tbuf, tsem, first_group + group)
+            for first in range(0, GROUP, BATCH):
+                entries = [backs_ref[part * SLOTS + group * GROUP + first + k] for k in range(BATCH)]
+                products = [
+                    jnp.dot(
+                        gbuf[pl.ds(pl.multiple_of((entry >> 7) * 16, 16), EDGE), :],
+                        tbuf[(first_group + group) * GROUP + first + k],
+                        preferred_element_type=F32,
+                    )
+                    for k, entry in enumerate(entries)
+                ]
+                for entry, product in zip(entries, products):
+                    acc[place(entry & 127), :] += product
+            return carry
+
+        lax.fori_loop(0, groups[which], body, 0)
+
+    if not chunk:
+
+        def store(at):
+            out_ref[at, :] = acc[at, :]
+
+        over_tiles(64, store)
+        return
+    for k in range(0, TERMS, 48):
+        terms = jnp.zeros((48, EDGE), F32)
         for owner in range(NY * NZH * NCO):
-            total += gbuf[pl.ds(owner * BLOCK0 + PARTS[0] * EDGE + k, rows), :].astype(F32)
-        cores = []
-        for core in range(NCO):
-            rings = []
-            for dy in range(NY):
-                first = second + (core * NY + dy) * NZH * BLOCK1 + k
-                rings.append(
-                    both_ways(
-                        [gbuf[pl.ds(first + dz * BLOCK1, rows), :].astype(F32) for dz in range(NZH)]
-                    )
-                )
-            cores.append(both_ways(rings))
-        return (total + (cores[0] + cores[1])).astype(BF)
-
-    for k in range(0, TERMS, 48):
-        terms = terms_of(k, 48)
+            terms += gbuf[pl.ds(owner * BLOCK + PARTS[1] * EDGE + k, 48), :].astype(F32)
         for owner in range(8):
-            out_ref[pl.ds(owner * SENT + 8 * EDGE + k, 48), :] = terms
+            out_ref[pl.ds(owner * SENT + 8 * EDGE + k, 48), :] = terms.astype(BF)
     for owner in range(8):
         for tile in range(8):
             at = pl.ds(owner * SENT + tile * EDGE, EDGE)
             out_ref[at, :] = acc[pl.ds((owner * 8 + tile) * EDGE, EDGE), :].astype(BF)
 
 
-def backward(backs, numbers, sources, tiles):
+def backward(chunk, lists, backs, numbers, sources, tiles, before):
     sizes = tuple(source.shape[0] for source in sources)
     return pl.pallas_call(
-        functools.partial(backward_kernel, sizes),
-        out_shape=shape_of(8 * SENT, BF),
-        in_specs=[in_smem()] * 2 + [in_any()] * (len(sizes) + 1),
+        functools.partial(backward_kernel, chunk, sizes),
+        out_shape=shape_of(8 * SENT, BF) if chunk else shape_of(64 * EDGE, F32),
+        in_specs=[in_smem()] * 3 + [in_any()] * (len(sizes) + 1 + len(before)),
         out_specs=in_vmem(),
         scratch_shapes=[
             pltpu.VMEM((sum(sizes), EDGE), BF),
-            pltpu.VMEM((tiles.shape[0], EDGE, EDGE), BF),
+            pltpu.VMEM((SLOTS + GROUP, EDGE, EDGE), BF),
             pltpu.VMEM((65 * EDGE, EDGE), F32),
             pltpu.SemaphoreType.DMA((len(sizes),)),
-            pltpu.SemaphoreType.DMA((SLOTS // GROUP,)),
+            pltpu.SemaphoreType.DMA((SLOTS // GROUP + 1,)),
+            pltpu.SemaphoreType.DMA((1,)),
         ],
         compiler_params=params(),
         name="backward",
-    )(backs, numbers, *sources, tiles)
+    )(lists, backs, numbers, *sources, tiles, *before)
 
 
 def last_kernel(got_ref, out_ref, weight_ref, bias_ref):
@@ -544,7 +545,7 @@
 
 def on_device(features, tiles, tile_rows, tile_cols, tile_count, weight, bias, cotangent):
     tile_set = tiles[0, 0]
-    part, entry, backs = slot_entries(tile_rows[0, 0], tile_cols[0, 0])
+    part, entry, back = slot_entries(tile_rows[0, 0], tile_cols[0, 0])
 
     mine = features
     beside = after(send_row(mine, dzl=1), entry)
@@ -553,7 +554,7 @@
     mine_far = send_row(mine_left, dx=1)
     beside_far = send_row(beside_right, dx=-1)
     pieces = (mine, beside, mine_right, beside_right, mine_far, beside_far, mine_left, beside_left)
-    lists, numbers = make_bins(after(tile_count, mine_left, beside_right), part, entry)
+    lists, backs, numbers = make_bins(after(tile_count, mine_left, beside_right), part, entry, back)
 
     latest = []
 
@@ -573,29 +574,31 @@
     for c in both:
         rings.append(ran(forward_keep(c, gate(lists), numbers, pieces, tile_set, got[c])))
     bias_row = bias.reshape(1, EDGE)
-    for axis in ("dy", "dzh"):
-        early = [(send_col(r[1], **{axis: 1}), send_col(r[2], **{axis: -1})) for r in rings]
-        late = []
-        for c in both:
-            on_right, on_left = ran(relay_middle(gate(rings[c][3]), rings[c][4], *early[c]))
-            late.append((send_col(on_right, **{axis: 1}), send_col(on_left, **{axis: -1})))
-        sums = [(rings[c][0],) + early[c] + late[c] for c in both]
-        if axis == "dy":
-            rings = [ran(ring_turn(gate(own), *others)) for own, *others in sums]
-    act, blocks = (), []
+    early = [(send_col(r[1], dy=1), send_col(r[2], dy=-1)) for r in rings]
+    late = []
+    for c in both:
+        on_right, on_left = ran(relay_middle(gate(rings[c][3]), rings[c][4], *early[c]))
+        late.append((send_col(on_right, dy=1), send_col(on_left, dy=-1)))
+    sums = []
+    for c in both:
+        own, *blocks = ran(ring_turn(gate(rings[c][0]), *early[c], *late[c]))
+        sums.append((own,) + tuple(send_col(block, dzh=n) for n, block in zip((1, 2, 3), blocks)))
+    before, blocks = (), []
     for c in both:
         own, *others = sums[c]
-        *act, block = ran(dense(c, (gate(own), *others), weight, bias_row, cotangent, act))
+        act, block, *terms = ran(dense(c, (gate(own), *others), weight, bias_row, cotangent, before))
+        before = (act, *terms)
         blocks.append(block)
 
-    gathered = lax.all_gather(blocks[0], "col", axis=0, tiled=True)
-    joined = join((blocks[1],) + around(blocks[1], "dzh"))
+    gathered = lax.all_gather(blocks[1], "col", axis=0, tiled=True)
+    joined = join((gate(blocks[0]),) + around(blocks[0], "dzh"))
     sources = (joined,) + around(joined, "dy")
     sources += tuple(send_col(source, dco=1) for source in sources)
-    partial = backward(backs, numbers, (gathered,) + sources, tile_set)
+    partial = backward(0, lists, backs, numbers, sources, tile_set, ())
+    partial = backward(1, lists, backs, numbers, (gathered,), tile_set, (partial,))
     got = lax.all_to_all(partial.reshape(8, SENT, EDGE), "row", 0, 0, tiled=True)
     grad_features, grad_weight, grad_bias = last(got.reshape(8 * SENT, EDGE))
-    return act[0], grad_features, grad_weight, grad_bias.reshape(EDGE)
+    return act, grad_features, grad_weight, grad_bias.reshape(EDGE)
 
 
 def solution(mesh):

time: 260 us -> 251 us (0.965); the launches traced: 255 us -> 250 us
  starting transfers between devices: 91.4 us -> 69.4 us
  waiting for transfers between devices: 34.5 us -> 51.3 us
    ppermute x31 -> x29, starting transfers between devices: 79.2 us -> 57.3 us  [send_col(): return lax.ppermute(value, 'col', col_perm(**step))]
    ppermute x31 -> x29, waiting for transfers between devices: 26.4 us -> 40.5 us  [send_col(): return lax.ppermute(value, 'col', col_perm(**step))]
    pallas_call x5 -> x6, Pallas kernels: 28.1 us -> 32.4 us  [the longest x2 22.4 us: backward(): pl.pallas_call(functools.partial(backward_kernel, chunk, sizes), out_shap...]
    pallas_call x4 -> x2, Pallas kernels: 8.24 us -> 4.73 us  [relay_middle(): pl.pallas_call(middle_kernel, out_shape=(shape_of(rest_right.shape[0], BF...]
    all_gather x1, waiting for transfers between devices: 0.01 us -> 3.14 us  [on_device(): gathered = lax.all_gather(blocks[1], 'col', axis=0, tiled=True)]
  transfers between devices with their start and end apart: 39 -> 37, of which waited for: 17 -> 19; matrix products, arithmetic and copies ran while one was open for 1% -> 1% of each run, Pallas kernels for 18% -> 21%
where the time goes in v1:
time: 251 us; the launch traced here: 250 us
  Pallas kernels  74.9 us (30%)
  starting transfers between devices  69.4 us (28%)
  waiting for transfers between devices  51.3 us (20%)
  blocking collectives  34.2 us (14%)
  between operations  14.9 us (6%)
  local copies, waits for them, and re-layouts  3.1 us (1%)
  other arithmetic  2.71 us (1%)
    ppermute x29, starting transfers between devices, send_col(): return lax.ppermute(value, 'col', col_perm(**step))  57.3 us
    ppermute x29, waiting for transfers between devices, send_col(): return lax.ppermute(value, 'col', col_perm(**step))  40.5 us
    all_to_all x1, blocking collectives, on_device(): lax.all_to_all(partial.reshape(8, SENT, EDGE), 'row', 0, 0, tiled=True)  34.2 us
    pallas_call x2, Pallas kernels, backward(): pl.pallas_call(functools.partial(backward_kernel, chunk, sizes), out_shap...  22.4 us
    pallas_call x2, Pallas kernels, forward_keep(): pl.pallas_call(functools.partial(forward_keep_kernel, part), out_shape=re...  15.3 us
    pallas_call x2, Pallas kernels, forward_send(): pl.pallas_call(functools.partial(forward_send_kernel, part), out_shape=sh...  13.8 us
    ppermute x7, starting transfers between devices, send_row(): return lax.ppermute(value, 'row', row_perm(**step))  12.1 us
    ppermute x7, waiting for transfers between devices, send_row(): return lax.ppermute(value, 'row', row_perm(**step))  7.59 us
  transfers between devices with their start and end apart: 37, of which 19 were waited for; matrix products, arithmetic and copies ran while one was open for 1% of the time, Pallas kernels for 21%

profile of v1, /device:TPU:1, one launch (start us, length us, event | category | flops | bytes accessed | tf_op | source)
XLA Modules:
  0.0 250.4 jit_solution(6578747586801364027)
XLA Ops:
  15.1 3.4 %collective-permute-start.2 = (bf16[1024,128]{1,0:T(8,128)(2,1)}, bf16[1024,128]{1,0:T(8,128)(2,1)}, u32[]{:S(2)}, u32[]{:S(2)}) collective-permute-start(bf16[1024,128]{1,0:T(8,128)(2,1)} %collective-permute-done.1.refs_1_), channel_id=1, source_target_pairs={{0,192},{32,224},{64,0},{96,32},{128,64},{160,96},{192,128},{224,1... | collective-permute-start | bytes 786440 | tf_op jit(solution)/shard_map/ppermute | solution.py:49
  20.0 3.1 %collective-permute-done.2.refs_3_ = bf16[1024,128]{1,0:T(8,128)(2,1)} collective-permute-done((bf16[1024,128]{1,0:T(8,128)(2,1)}, bf16[1024,128]{1,0:T(8,128)(2,1)}, u32[]{:S(2)}, u32[]{:S(2)}) %collective-permute-start.2) | collective-permute-done | bytes 262176 | tf_op jit(solution)/shard_map/ppermute | solution.py:49
  23.1 3.4 %collective-permute-start.5 = (bf16[1024,128]{1,0:T(8,128)(2,1)}, bf16[1024,128]{1,0:T(8,128)(2,1)}, u32[]{:S(2)}, u32[]{:S(2)}) collective-permute-start(bf16[1024,128]{1,0:T(8,128)(2,1)} %collective-permute-done.2.refs_3_), channel_id=1, source_target_pairs={{0,192},{32,224},{64,0},{96,32},{128,64},{160,96},{192,128},{224,1... | collective-permute-start | bytes 786440 | tf_op jit(solution)/shard_map/ppermute | solution.py:49
  27.1 4.0 %bins.1 = (s32[1536]{0:T(1024)}, s32[1536]{0:T(1024)}, s32[4]{0:T(128)}) custom-call(s32[1,1]{1,0:T(1,128)S(6)} %copy.12.count_ref, s32[368]{0:T(512)} %get-tuple-element.99.part_ref, s32[368]{0:T(512)} %get-tuple-element.98.entry_ref, s32[368]{0:T(512)} %get-tuple-element.97.back_ref), custom_call_target="tpu_custom_call" | custom-call | tf_op jit(solution)/shard_map/bins/pallas_call | solution.py:122
  34.3 7.0 %forward_send.2 = bf16[8192,128]{1,0:T(8,128)(2,1)} custom-call(s32[1536]{0:T(1024)} %get-tuple-element.56.list_ref, s32[4]{0:T(128)} %get-tuple-element.52.number_ref, bf16[1024,128]{1,0:T(8,128)(2,1)} %refs_0_.7, bf16[1024,128]{1,0:T(8,128)(2,1)} %collective-permute-done.1.refs_1_, bf16[1024,128]{1,0:T(8,128)(2,1)} %collective-permute-done.3.refs_2_, ...), custom_call_target="tpu_custom_call" | custom-call | tf_op jit(solution)/shard_map/forward_send/pallas_call | solution.py:285
  43.0 6.7 %forward_send.3 = bf16[8192,128]{1,0:T(8,128)(2,1)} custom-call(s32[1536]{0:T(1024)} %get-tuple-element.56.list_ref, s32[4]{0:T(128)} %get-tuple-element.52.number_ref, bf16[1024,128]{1,0:T(8,128)(2,1)} %refs_0_.7, bf16[1024,128]{1,0:T(8,128)(2,1)} %collective-permute-done.1.refs_1_, bf16[1024,128]{1,0:T(8,128)(2,1)} %collective-permute-done.3.refs_2_, ...), custom_call_target="tpu_custom_call" | custom-call | tf_op jit(solution)/shard_map/forward_send/pallas_call | solution.py:285
  49.8 7.7 %forward_keep.2 = (f32[2048,128]{1,0:T(8,128)}, bf16[2048,128]{1,0:T(8,128)(2,1)}, bf16[2048,128]{1,0:T(8,128)(2,1)}, f32[1024,128]{1,0:T(8,128)}, f32[1024,128]{1,0:T(8,128)}) custom-call(s32[1536]{0:T(1024)} %get-tuple-element.56.list_ref, s32[4]{0:T(128)} %get-tuple-element.52.number_ref, bf16[1024,128]{1,0:T(8,128)(2,1)} %refs_0_.7, ...), custom_call_target="tpu_custom_call" | custom-call | tf_op jit(solution)/shard_map/forward_keep/pallas_call | solution.py:297
  57.6 4.9 %collective-permute-start.10 = (bf16[2048,128]{1,0:T(8,128)(2,1)}, bf16[2048,128]{1,0:T(8,128)(2,1)}, u32[]{:S(2)}, u32[]{:S(2)}) collective-permute-start(bf16[2048,128]{1,0:T(8,128)(2,1)} %get-tuple-element.63), channel_id=1, source_target_pairs={{0,24},{1,25},{2,26},{3,27},{4,28},{5,29},{6,30},{7,31},{8,0},{9,1... | collective-permute-start | bytes 1572872 | tf_op jit(solution)/shard_map/ppermute | solution.py:53
  62.5 7.6 %forward_keep.3 = (f32[2048,128]{1,0:T(8,128)}, bf16[2048,128]{1,0:T(8,128)(2,1)}, bf16[2048,128]{1,0:T(8,128)(2,1)}, f32[1024,128]{1,0:T(8,128)}, f32[1024,128]{1,0:T(8,128)}) custom-call(s32[1536]{0:T(1024)} %get-tuple-element.56.list_ref, s32[4]{0:T(128)} %get-tuple-element.52.number_ref, bf16[1024,128]{1,0:T(8,128)(2,1)} %refs_0_.7, ...), custom_call_target="tpu_custom_call" | custom-call | tf_op jit(solution)/shard_map/forward_keep/pallas_call | solution.py:297
  74.3 3.5 %collective-permute-done.9.from_left.refs_1_ = bf16[2048,128]{1,0:T(8,128)(2,1)} collective-permute-done((bf16[2048,128]{1,0:T(8,128)(2,1)}, bf16[2048,128]{1,0:T(8,128)(2,1)}, u32[]{:S(2)}, u32[]{:S(2)}) %collective-permute-start.9) | collective-permute-done | bytes 524320 | tf_op jit(solution)/shard_map/ppermute | solution.py:53
  82.9 6.2 %collective-permute-done.11.from_left.refs_1_ = bf16[2048,128]{1,0:T(8,128)(2,1)} collective-permute-done((bf16[2048,128]{1,0:T(8,128)(2,1)}, bf16[2048,128]{1,0:T(8,128)(2,1)}, u32[]{:S(2)}, u32[]{:S(2)}) %collective-permute-start.11) | collective-permute-done | bytes 524320 | tf_op jit(solution)/shard_map/ppermute | solution.py:53
  97.3 6.4 %collective-permute-start.18 = (bf16[512,128]{1,0:T(8,128)(2,1)}, bf16[512,128]{1,0:T(8,128)(2,1)}, u32[]{:S(2)}, u32[]{:S(2)}) collective-permute-start(bf16[512,128]{1,0:T(8,128)(2,1)} %get-tuple-element.78), channel_id=1, source_target_pairs={{0,4},{1,5},{2,6},{3,7},{4,0},{5,1},{6,2},{7,3},{8,12},{9,13},{10,... | collective-permute-start | bytes 393224 | tf_op jit(solution)/shard_map/ppermute | solution.py:53
  109.6 3.5 %collective-permute-start.22 = (bf16[512,128]{1,0:T(8,128)(2,1)}, bf16[512,128]{1,0:T(8,128)(2,1)}, u32[]{:S(2)}, u32[]{:S(2)}) collective-permute-start(bf16[512,128]{1,0:T(8,128)(2,1)} %get-tuple-element.84), channel_id=1, source_target_pairs={{0,6},{1,7},{2,0},{3,1},{4,2},{5,3},{6,4},{7,5},{8,14},{9,15},{10,... | collective-permute-start | bytes 393224 | tf_op jit(solution)/shard_map/ppermute | solution.py:53
  113.1 3.3 %collective-permute-done.19.refs_3_ = bf16[512,128]{1,0:T(8,128)(2,1)} collective-permute-done((bf16[512,128]{1,0:T(8,128)(2,1)}, bf16[512,128]{1,0:T(8,128)(2,1)}, u32[]{:S(2)}, u32[]{:S(2)}) %collective-permute-start.19) | collective-permute-done | bytes 131104 | tf_op jit(solution)/shard_map/ppermute | solution.py:53
  126.4 3.5 %collective-permute-start.24 = (bf16[512,128]{1,0:T(8,128)(2,1)}, bf16[512,128]{1,0:T(8,128)(2,1)S(1)}, u32[]{:S(2)}, u32[]{:S(2)}) collective-permute-start(bf16[512,128]{1,0:T(8,128)(2,1)} %get-tuple-element.90.refs_0_), channel_id=1, source_target_pairs={{0,2},{1,3},{2,4},{3,5},{4,6},{5,7},{6,0},{7,1},{8,10},{9,11},{10,... | collective-permute-start | bytes 393224 | tf_op jit(solution)/shard_map/ppermute | solution.py:53
  131.2 3.7 %collective-permute-done.24.refs_4_ = bf16[512,128]{1,0:T(8,128)(2,1)S(1)} collective-permute-done((bf16[512,128]{1,0:T(8,128)(2,1)}, bf16[512,128]{1,0:T(8,128)(2,1)S(1)}, u32[]{:S(2)}, u32[]{:S(2)}) %collective-permute-start.24) | collective-permute-done | bytes 131104 | tf_op jit(solution)/shard_map/ppermute | solution.py:53
  136.3 3.6 %collective-permute-start.26 = (bf16[256,128]{1,0:T(8,128)(2,1)S(1)}, bf16[256,128]{1,0:T(8,128)(2,1)}, u32[]{:S(2)}, u32[]{:S(2)}) collective-permute-start(bf16[256,128]{1,0:T(8,128)(2,1)S(1)} %slice.17), channel_id=1, source_target_pairs={{0,6},{1,7},{2,0},{3,1},{4,2},{5,3},{6,4},{7,5},{8,14},{9,15},{10,... | collective-permute-start | bytes 196616 | tf_op jit(solution)/shard_map/ppermute | solution.py:53
  143.2 3.7 %collective-permute-start.28 = (bf16[2048,128]{1,0:T(8,128)(2,1)}, bf16[2048,128]{1,0:T(8,128)(2,1)S(1)}, u32[]{:S(2)}, u32[]{:S(2)}) collective-permute-start(bf16[2048,128]{1,0:T(8,128)(2,1)} %join.1.refs_0_), channel_id=1, source_target_pairs={{0,8},{1,9},{2,10},{3,11},{4,12},{5,13},{6,14},{7,15},{8,16},{9,17... | collective-permute-start | bytes 1572872 | tf_op jit(solution)/shard_map/ppermute | solution.py:53
  151.6 11.6 %collective-permute-done.28.refs_4_ = bf16[2048,128]{1,0:T(8,128)(2,1)S(1)} collective-permute-done((bf16[2048,128]{1,0:T(8,128)(2,1)}, bf16[2048,128]{1,0:T(8,128)(2,1)S(1)}, u32[]{:S(2)}, u32[]{:S(2)}) %collective-permute-start.28) | collective-permute-done | bytes 524320 | tf_op jit(solution)/shard_map/ppermute | solution.py:53
  170.7 6.0 %collective-permute-start.33 = (bf16[1024,128]{1,0:T(8,128)(2,1)S(1)}, bf16[1024,128]{1,0:T(8,128)(2,1)S(1)}, u32[]{:S(2)}, u32[]{:S(2)}) collective-permute-start(bf16[1024,128]{1,0:T(8,128)(2,1)S(1)} %collective-permute-done.29.refs_2_), channel_id=1, source_target_pairs={{0,1},{1,0},{2,3},{3,2},{4,5},{5,4},{6,7},{7,6},{8,9},{9,8},{10,11... | collective-permute-start | bytes 786440 | tf_op jit(solution)/shard_map/ppermute | solution.py:53
  181.1 11.3 %backward.2.refs_2_ = f32[8192,128]{1,0:T(8,128)} custom-call(s32[1536]{0:T(1024)} %get-tuple-element.56.list_ref, s32[1536]{0:T(1024)} %get-tuple-element.87.backs_ref, s32[4]{0:T(128)} %get-tuple-element.52.number_ref, bf16[2048,128]{1,0:T(8,128)(2,1)} %join.1.refs_0_, bf16[2048,128]{1,0:T(8,128)(2,1)} %copy-done.1, bf16[1024,128]{1,0:T(8,128)(2,1)} %copy-done.7, ...), custom_call_target="tpu_custom_call" | custom-call | tf_op jit(solution)/shard_map/backward/pallas_call | solution.py:494
  192.4 3.1 %all-gather.2.cloned.1.call-done.refs_0_ = bf16[20992,128]{1,0:T(8,128)(2,1)} async-done(((bf16[656,128]{1,0:T(8,128)(2,1)}), bf16[20992,128]{1,0:T(8,128)(2,1)}) %all-gather.2.cloned.1.call-update) | async-done | bytes 5373968 | tf_op jit(solution)/shard_map/all_gather | solution.py:593
  195.5 11.1 %backward.3 = bf16[9344,128]{1,0:T(8,128)(2,1)} custom-call(s32[1536]{0:T(1024)} %get-tuple-element.56.list_ref, s32[1536]{0:T(1024)} %get-tuple-element.87.backs_ref, s32[4]{0:T(128)} %get-tuple-element.52.number_ref, bf16[20992,128]{1,0:T(8,128)(2,1)} %all-gather.2.cloned.1.call-done.refs_0_, bf16[368,128,128]{2,1,0:T(8,128)(2,1)} %bitcast.10, ...), custom_call_target="tpu_custom_call" | custom-call | tf_op jit(solution)/shard_map/backward/pallas_call | solution.py:494
  206.7 34.2 %all_to_all.5 = bf16[8,1168,128]{2,1,0:T(8,128)(2,1)} all-to-all(bf16[8,1168,128]{2,1,0:T(8,128)(2,1)} %bitcast.11), channel_id=1, replica_groups=mesh['row'=8,'col'=32] {'row'}, dimensions={0} | all-to-all | bytes 4784128 | tf_op jit(solution)/shard_map/all_to_all | solution.py:599
  (97 shorter events, 72.9 us)
Async XLA Ops:
  7.2 188.4 %all-gather.2.cloned.1.call-start = ((), (), s32[]{:S(2)}) async-start(), calls=%async_computation.1 | async-start | bytes 5541888 | tf_op jit(solution)/shard_map/all_gather | solution.py:593
  18.5 12.6 %collective-permute-start.3 = (bf16[1024,128]{1,0:T(8,128)(2,1)}, bf16[1024,128]{1,0:T(8,128)(2,1)}, u32[]{:S(2)}, u32[]{:S(2)}) collective-permute-start(bf16[1024,128]{1,0:T(8,128)(2,1)} %refs_0_.7), channel_id=1, source_target_pairs={{0,192},{32,224},{64,0},{96,32},{128,64},{160,96},{192,128},{224,1... | collective-permute-start | bytes 786440 | tf_op jit(solution)/shard_map/ppermute | solution.py:49
  19.0 12.1 %collective-permute-start.6 = (bf16[1024,128]{1,0:T(8,128)(2,1)}, bf16[1024,128]{1,0:T(8,128)(2,1)}, u32[]{:S(2)}, u32[]{:S(2)}) collective-permute-start(bf16[1024,128]{1,0:T(8,128)(2,1)} %collective-permute-done.1.refs_1_), channel_id=1, source_target_pairs={{0,64},{32,96},{64,128},{96,160},{128,192},{160,224},{192,0},{224,... | collective-permute-start | bytes 786440 | tf_op jit(solution)/shard_map/ppermute | solution.py:49
  19.9 12.1 %collective-permute-start.4 = (bf16[1024,128]{1,0:T(8,128)(2,1)}, bf16[1024,128]{1,0:T(8,128)(2,1)}, u32[]{:S(2)}, u32[]{:S(2)}) collective-permute-start(bf16[1024,128]{1,0:T(8,128)(2,1)} %collective-permute-done.refs_6_), channel_id=1, source_target_pairs={{0,64},{32,96},{64,128},{96,160},{128,192},{160,224},{192,0},{224,... | collective-permute-start | bytes 786440 | tf_op jit(solution)/shard_map/ppermute | solution.py:49
  49.7 12.8 %collective-permute-start.8 = (bf16[8192,128]{1,0:T(8,128)(2,1)}, bf16[8192,128]{1,0:T(8,128)(2,1)}, u32[]{:S(2)}, u32[]{:S(2)}) collective-permute-start(bf16[8192,128]{1,0:T(8,128)(2,1)} %forward_send.3), channel_id=1, source_target_pairs={{0,1},{1,0},{2,3},{3,2},{4,5},{5,4},{6,7},{7,6},{8,9},{9,8},{10,11... | collective-permute-start | bytes 6291464 | tf_op jit(solution)/shard_map/ppermute | solution.py:53
  57.6 16.8 %collective-permute-start.10 = (bf16[2048,128]{1,0:T(8,128)(2,1)}, bf16[2048,128]{1,0:T(8,128)(2,1)}, u32[]{:S(2)}, u32[]{:S(2)}) collective-permute-start(bf16[2048,128]{1,0:T(8,128)(2,1)} %get-tuple-element.63), channel_id=1, source_target_pairs={{0,24},{1,25},{2,26},{3,27},{4,28},{5,29},{6,30},{7,31},{8,0},{9,1... | collective-permute-start | bytes 1572872 | tf_op jit(solution)/shard_map/ppermute | solution.py:53
  62.5 15.4 %collective-permute-start.9 = (bf16[2048,128]{1,0:T(8,128)(2,1)}, bf16[2048,128]{1,0:T(8,128)(2,1)}, u32[]{:S(2)}, u32[]{:S(2)}) collective-permute-start(bf16[2048,128]{1,0:T(8,128)(2,1)} %get-tuple-element.62), channel_id=1, source_target_pairs={{0,8},{1,9},{2,10},{3,11},{4,12},{5,13},{6,14},{7,15},{8,16},{9,17... | collective-permute-start | bytes 1572872 | tf_op jit(solution)/shard_map/ppermute | solution.py:53
  70.0 19.1 %collective-permute-start.11 = (bf16[2048,128]{1,0:T(8,128)(2,1)}, bf16[2048,128]{1,0:T(8,128)(2,1)}, u32[]{:S(2)}, u32[]{:S(2)}) collective-permute-start(bf16[2048,128]{1,0:T(8,128)(2,1)} %get-tuple-element.67), channel_id=1, source_target_pairs={{0,8},{1,9},{2,10},{3,11},{4,12},{5,13},{6,14},{7,15},{8,16},{9,17... | collective-permute-start | bytes 1572872 | tf_op jit(solution)/shard_map/ppermute | solution.py:53
  70.1 19.0 %collective-permute-start.12 = (bf16[2048,128]{1,0:T(8,128)(2,1)}, bf16[2048,128]{1,0:T(8,128)(2,1)}, u32[]{:S(2)}, u32[]{:S(2)}) collective-permute-start(bf16[2048,128]{1,0:T(8,128)(2,1)} %get-tuple-element.68), channel_id=1, source_target_pairs={{0,24},{1,25},{2,26},{3,27},{4,28},{5,29},{6,30},{7,31},{8,0},{9,1... | collective-permute-start | bytes 1572872 | tf_op jit(solution)/shard_map/ppermute | solution.py:53
  80.3 14.5 %collective-permute-start.13 = (bf16[1024,128]{1,0:T(8,128)(2,1)}, bf16[1024,128]{1,0:T(8,128)(2,1)}, u32[]{:S(2)}, u32[]{:S(2)}) collective-permute-start(bf16[1024,128]{1,0:T(8,128)(2,1)} %get-tuple-element.64), channel_id=1, source_target_pairs={{0,8},{1,9},{2,10},{3,11},{4,12},{5,13},{6,14},{7,15},{8,16},{9,17... | collective-permute-start | bytes 786440 | tf_op jit(solution)/shard_map/ppermute | solution.py:53
  80.3 14.5 %collective-permute-start.14 = (bf16[1024,128]{1,0:T(8,128)(2,1)}, bf16[1024,128]{1,0:T(8,128)(2,1)}, u32[]{:S(2)}, u32[]{:S(2)}) collective-permute-start(bf16[1024,128]{1,0:T(8,128)(2,1)} %get-tuple-element.71), channel_id=1, source_target_pairs={{0,24},{1,25},{2,26},{3,27},{4,28},{5,29},{6,30},{7,31},{8,0},{9,1... | collective-permute-start | bytes 786440 | tf_op jit(solution)/shard_map/ppermute | solution.py:53
  91.5 13.5 %collective-permute-start.15 = (bf16[1024,128]{1,0:T(8,128)(2,1)}, bf16[1024,128]{1,0:T(8,128)(2,1)}, u32[]{:S(2)}, u32[]{:S(2)}) collective-permute-start(bf16[1024,128]{1,0:T(8,128)(2,1)} %get-tuple-element.69), channel_id=1, source_target_pairs={{0,8},{1,9},{2,10},{3,11},{4,12},{5,13},{6,14},{7,15},{8,16},{9,17... | collective-permute-start | bytes 786440 | tf_op jit(solution)/shard_map/ppermute | solution.py:53
  91.5 13.5 %collective-permute-start.16 = (bf16[1024,128]{1,0:T(8,128)(2,1)}, bf16[1024,128]{1,0:T(8,128)(2,1)}, u32[]{:S(2)}, u32[]{:S(2)}) collective-permute-start(bf16[1024,128]{1,0:T(8,128)(2,1)} %get-tuple-element.74), channel_id=1, source_target_pairs={{0,24},{1,25},{2,26},{3,27},{4,28},{5,29},{6,30},{7,31},{8,0},{9,1... | collective-permute-start | bytes 786440 | tf_op jit(solution)/shard_map/ppermute | solution.py:53
  97.3 12.3 %collective-permute-start.17 = (bf16[512,128]{1,0:T(8,128)(2,1)}, bf16[512,128]{1,0:T(8,128)(2,1)}, u32[]{:S(2)}, u32[]{:S(2)}) collective-permute-start(bf16[512,128]{1,0:T(8,128)(2,1)} %get-tuple-element.77), channel_id=1, source_target_pairs={{0,2},{1,3},{2,4},{3,5},{4,6},{5,7},{6,0},{7,1},{8,10},{9,11},{10,... | collective-permute-start | bytes 393224 | tf_op jit(solution)/shard_map/ppermute | solution.py:53
  97.3 15.8 %collective-permute-start.18 = (bf16[512,128]{1,0:T(8,128)(2,1)}, bf16[512,128]{1,0:T(8,128)(2,1)}, u32[]{:S(2)}, u32[]{:S(2)}) collective-permute-start(bf16[512,128]{1,0:T(8,128)(2,1)} %get-tuple-element.78), channel_id=1, source_target_pairs={{0,4},{1,5},{2,6},{3,7},{4,0},{5,1},{6,2},{7,3},{8,12},{9,13},{10,... | collective-permute-start | bytes 393224 | tf_op jit(solution)/shard_map/ppermute | solution.py:53
  103.7 12.7 %collective-permute-start.19 = (bf16[512,128]{1,0:T(8,128)(2,1)}, bf16[512,128]{1,0:T(8,128)(2,1)}, u32[]{:S(2)}, u32[]{:S(2)}) collective-permute-start(bf16[512,128]{1,0:T(8,128)(2,1)} %get-tuple-element.79), channel_id=1, source_target_pairs={{0,6},{1,7},{2,0},{3,1},{4,2},{5,3},{6,4},{7,5},{8,14},{9,15},{10,... | collective-permute-start | bytes 393224 | tf_op jit(solution)/shard_map/ppermute | solution.py:53
  108.6 12.8 %collective-permute-start.21 = (bf16[512,128]{1,0:T(8,128)(2,1)}, bf16[512,128]{1,0:T(8,128)(2,1)}, u32[]{:S(2)}, u32[]{:S(2)}) collective-permute-start(bf16[512,128]{1,0:T(8,128)(2,1)} %get-tuple-element.83), channel_id=1, source_target_pairs={{0,4},{1,5},{2,6},{3,7},{4,0},{5,1},{6,2},{7,3},{8,12},{9,13},{10,... | collective-permute-start | bytes 393224 | tf_op jit(solution)/shard_map/ppermute | solution.py:53
  109.6 14.3 %collective-permute-start.22 = (bf16[512,128]{1,0:T(8,128)(2,1)}, bf16[512,128]{1,0:T(8,128)(2,1)}, u32[]{:S(2)}, u32[]{:S(2)}) collective-permute-start(bf16[512,128]{1,0:T(8,128)(2,1)} %get-tuple-element.84), channel_id=1, source_target_pairs={{0,6},{1,7},{2,0},{3,1},{4,2},{5,3},{6,4},{7,5},{8,14},{9,15},{10,... | collective-permute-start | bytes 393224 | tf_op jit(solution)/shard_map/ppermute | solution.py:53
  143.2 19.9 %collective-permute-start.28 = (bf16[2048,128]{1,0:T(8,128)(2,1)}, bf16[2048,128]{1,0:T(8,128)(2,1)S(1)}, u32[]{:S(2)}, u32[]{:S(2)}) collective-permute-start(bf16[2048,128]{1,0:T(8,128)(2,1)} %join.1.refs_0_), channel_id=1, source_target_pairs={{0,8},{1,9},{2,10},{3,11},{4,12},{5,13},{6,14},{7,15},{8,16},{9,17... | collective-permute-start | bytes 1572872 | tf_op jit(solution)/shard_map/ppermute | solution.py:53
  146.9 16.3 %collective-permute-start.27 = (bf16[2048,128]{1,0:T(8,128)(2,1)}, bf16[2048,128]{1,0:T(8,128)(2,1)S(1)}, u32[]{:S(2)}, u32[]{:S(2)}) collective-permute-start(bf16[2048,128]{1,0:T(8,128)(2,1)} %join.1.refs_0_), channel_id=1, source_target_pairs={{0,24},{1,25},{2,26},{3,27},{4,28},{5,29},{6,30},{7,31},{8,0},{9,1... | collective-permute-start | bytes 1572872 | tf_op jit(solution)/shard_map/ppermute | solution.py:53
  150.0 28.9 %collective-permute-start.31 = (bf16[2048,128]{1,0:T(8,128)(2,1)}, bf16[2048,128]{1,0:T(8,128)(2,1)S(1)}, u32[]{:S(2)}, u32[]{:S(2)}) collective-permute-start(bf16[2048,128]{1,0:T(8,128)(2,1)} %join.1.refs_0_), channel_id=1, source_target_pairs={{0,1},{1,0},{2,3},{3,2},{4,5},{5,4},{6,7},{7,6},{8,9},{9,8},{10,11... | collective-permute-start | bytes 1572872 | tf_op jit(solution)/shard_map/ppermute | solution.py:53
  163.3 15.6 %collective-permute-start.32 = (bf16[2048,128]{1,0:T(8,128)(2,1)S(1)}, bf16[2048,128]{1,0:T(8,128)(2,1)S(1)}, u32[]{:S(2)}, u32[]{:S(2)}) collective-permute-start(bf16[2048,128]{1,0:T(8,128)(2,1)S(1)} %collective-permute-done.27.refs_1_), channel_id=1, source_target_pairs={{0,1},{1,0},{2,3},{3,2},{4,5},{5,4},{6,7},{7,6},{8,9},{9,8},{10,11... | collective-permute-start | bytes 1572872 | tf_op jit(solution)/shard_map/ppermute | solution.py:53
  164.9 14.1 %collective-permute-start.35 = (bf16[2048,128]{1,0:T(8,128)(2,1)S(1)}, bf16[2048,128]{1,0:T(8,128)(2,1)S(1)}, u32[]{:S(2)}, u32[]{:S(2)}) collective-permute-start(bf16[2048,128]{1,0:T(8,128)(2,1)S(1)} %collective-permute-done.28.refs_4_), channel_id=1, source_target_pairs={{0,1},{1,0},{2,3},{3,2},{4,5},{5,4},{6,7},{7,6},{8,9},{9,8},{10,11... | collective-permute-start | bytes 1572872 | tf_op jit(solution)/shard_map/ppermute | solution.py:53
  165.4 12.1 %collective-permute-start.30 = (bf16[1024,128]{1,0:T(8,128)(2,1)S(1)}, bf16[1024,128]{1,0:T(8,128)(2,1)S(1)}, u32[]{:S(2)}, u32[]{:S(2)}) collective-permute-start(bf16[1024,128]{1,0:T(8,128)(2,1)S(1)} %slice.19), channel_id=1, source_target_pairs={{0,24},{1,25},{2,26},{3,27},{4,28},{5,29},{6,30},{7,31},{8,0},{9,1... | collective-permute-start | bytes 786440 | tf_op jit(solution)/shard_map/ppermute | solution.py:53
  (24 other events, 135.4 us)
Sparse Core Ops, SparseCore 0:
  126.5 68.9 all-gather.1

commit v2 on v1

--- a/solution.py
+++ b/solution.py
@@ -228,7 +228,8 @@
 
 def forward_keep_kernel(part, list_ref, number_ref, *refs):
     pieces, refs = refs[:8], refs[8:]
-    tiles_ref, got_ref, own, to_right, to_left, rest_right, rest_left, xbuf, tbuf, acc, xsem, tsem = refs
+    tiles_ref, got_ref, outs = refs[0], refs[1], refs[2:-5]
+    xbuf, tbuf, acc, xsem, tsem = refs[-5:]
 
     def start():
         def load(at):
@@ -237,7 +238,8 @@
         over_tiles(AREAS[part], load)
 
     forward_sum(2 * part, list_ref, number_ref, pieces, tiles_ref, xbuf, tbuf, acc, xsem, tsem, start)
-    split_relay(lambda k, rows: acc[pl.ds(k, rows), :], own, to_right, to_left, rest_right, rest_left)
+    split = split_direct if part else split_relay
+    split(lambda k, rows: acc[pl.ds(k, rows), :], *outs)
 
 
 def split_relay(read, own, to_right, to_left, rest_right, rest_left):
@@ -296,9 +298,9 @@
 def forward_keep(part, lists, numbers, pieces, tiles, got):
     return pl.pallas_call(
         functools.partial(forward_keep_kernel, part),
-        out_shape=relay_shapes(AREAS[part] * EDGE // 4),
+        out_shape=(direct_shapes if part else relay_shapes)(AREAS[part] * EDGE // 4),
         in_specs=[in_smem()] * 2 + [in_any()] * 9 + [in_vmem()],
-        out_specs=(in_vmem(),) * 5,
+        out_specs=(in_vmem(),) * (4 if part else 5),
         scratch_shapes=forward_scratch(part),
         compiler_params=params(),
         name="forward_keep",
@@ -346,14 +348,16 @@
 
 
 def turn_kernel(*refs):
-    split_direct(relay_total(*refs[:5]), *refs[5:])
+    values, outs = refs[:-4], refs[-4:]
+    read = relay_total(*values) if len(values) == 5 else direct_total(values[0], values[1:])
+    split_direct(read, *outs)
 
 
 def ring_turn(*values):
     return pl.pallas_call(
         turn_kernel,
         out_shape=direct_shapes(values[0].shape[0] // 4),
-        in_specs=[in_vmem()] * 5,
+        in_specs=[in_vmem()] * len(values),
         out_specs=(in_vmem(),) * 4,
         compiler_params=params(),
         name="turn",
@@ -574,14 +578,14 @@
     for c in both:
         rings.append(ran(forward_keep(c, gate(lists), numbers, pieces, tile_set, got[c])))
     bias_row = bias.reshape(1, EDGE)
-    early = [(send_col(r[1], dy=1), send_col(r[2], dy=-1)) for r in rings]
-    late = []
-    for c in both:
-        on_right, on_left = ran(relay_middle(gate(rings[c][3]), rings[c][4], *early[c]))
-        late.append((send_col(on_right, dy=1), send_col(on_left, dy=-1)))
+    own, to_right, to_left, rest_right, rest_left = rings[0]
+    early = (send_col(to_right, dy=1), send_col(to_left, dy=-1))
+    straight = tuple(send_col(block, dy=n) for n, block in zip((1, 2, 3), rings[1][1:]))
+    on_right, on_left = ran(relay_middle(gate(rest_right), rest_left, *early))
+    late = (send_col(on_right, dy=1), send_col(on_left, dy=-1))
     sums = []
-    for c in both:
-        own, *blocks = ran(ring_turn(gate(rings[c][0]), *early[c], *late[c]))
+    for own, came in ((own, early + late), (rings[1][0], straight)):
+        own, *blocks = ran(ring_turn(gate(own), *came))
         sums.append((own,) + tuple(send_col(block, dzh=n) for n, block in zip((1, 2, 3), blocks)))
     before, blocks = (), []
     for c in both:

time: 251 us -> 261 us (1.040); the launches traced: 250 us -> 257 us
  waiting for transfers between devices: 51.3 us -> 61.5 us
  Pallas kernels: 74.9 us -> 66.5 us
  starting transfers between devices: 69.4 us -> 75.9 us
    ppermute x29 -> x28, waiting for transfers between devices: 40.5 us -> 50 us  [send_col(): return lax.ppermute(value, 'col', col_perm(**step))]
    ppermute x29 -> x28, starting transfers between devices: 57.3 us -> 63.8 us  [send_col(): return lax.ppermute(value, 'col', col_perm(**step))]
    pallas_call x2, Pallas kernels: 22.4 us -> 19.8 us  [backward(): pl.pallas_call(functools.partial(backward_kernel, chunk, sizes), out_shap...]
  transfers between devices with their start and end apart: 37 -> 36, of which waited for: 19 -> 17; matrix products, arithmetic and copies ran while one was open for 1% -> 1% of each run, Pallas kernels for 21% -> 17%
where the time goes in v2:
time: 261 us; the launch traced here: 257 us
  starting transfers between devices  75.9 us (29%)
  Pallas kernels  66.5 us (25%)
  waiting for transfers between devices  61.5 us (24%)
  blocking collectives  32.9 us (13%)
  between operations  14.9 us (6%)
  local copies, waits for them, and re-layouts  2.91 us (1%)
  other arithmetic  2.73 us (1%)
    ppermute x28, starting transfers between devices, send_col(): return lax.ppermute(value, 'col', col_perm(**step))  63.8 us
    ppermute x28, waiting for transfers between devices, send_col(): return lax.ppermute(value, 'col', col_perm(**step))  50 us
    all_to_all x1, blocking collectives, on_device(): lax.all_to_all(partial.reshape(8, SENT, EDGE), 'row', 0, 0, tiled=True)  32.9 us
    pallas_call x2, Pallas kernels, backward(): pl.pallas_call(functools.partial(backward_kernel, chunk, sizes), out_shap...  19.8 us
    pallas_call x2, Pallas kernels, forward_keep(): pl.pallas_call(functools.partial(forward_keep_kernel, part), out_shape=(d...  13.6 us
    pallas_call x2, Pallas kernels, forward_send(): pl.pallas_call(functools.partial(forward_send_kernel, part), out_shape=sh...  12.8 us
    ppermute x7, starting transfers between devices, send_row(): return lax.ppermute(value, 'row', row_perm(**step))  12.1 us
    ppermute x7, waiting for transfers between devices, send_row(): return lax.ppermute(value, 'row', row_perm(**step))  8.19 us
  transfers between devices with their start and end apart: 36, of which 17 were waited for; matrix products, arithmetic and copies ran while one was open for 1% of the time, Pallas kernels for 17%

profile of v2, /device:TPU:1, one launch (start us, length us, event | category | flops | bytes accessed | tf_op | source)
XLA Modules:
  0.0 257.4 jit_solution(14091044819469676366)
XLA Ops:
  15.1 3.4 %collective-permute-start.2 = (bf16[1024,128]{1,0:T(8,128)(2,1)}, bf16[1024,128]{1,0:T(8,128)(2,1)}, u32[]{:S(2)}, u32[]{:S(2)}) collective-permute-start(bf16[1024,128]{1,0:T(8,128)(2,1)} %collective-permute-done.1.refs_1_), channel_id=1, source_target_pairs={{0,192},{32,224},{64,0},{96,32},{128,64},{160,96},{192,128},{224,1... | collective-permute-start | bytes 786440 | tf_op jit(solution)/shard_map/ppermute | solution.py:49
  20.0 3.1 %collective-permute-done.2.refs_3_ = bf16[1024,128]{1,0:T(8,128)(2,1)} collective-permute-done((bf16[1024,128]{1,0:T(8,128)(2,1)}, bf16[1024,128]{1,0:T(8,128)(2,1)}, u32[]{:S(2)}, u32[]{:S(2)}) %collective-permute-start.2) | collective-permute-done | bytes 262176 | tf_op jit(solution)/shard_map/ppermute | solution.py:49
  23.1 3.4 %collective-permute-start.5 = (bf16[1024,128]{1,0:T(8,128)(2,1)}, bf16[1024,128]{1,0:T(8,128)(2,1)}, u32[]{:S(2)}, u32[]{:S(2)}) collective-permute-start(bf16[1024,128]{1,0:T(8,128)(2,1)} %collective-permute-done.2.refs_3_), channel_id=1, source_target_pairs={{0,192},{32,224},{64,0},{96,32},{128,64},{160,96},{192,128},{224,1... | collective-permute-start | bytes 786440 | tf_op jit(solution)/shard_map/ppermute | solution.py:49
  27.1 3.4 %bins.1 = (s32[1536]{0:T(1024)}, s32[1536]{0:T(1024)}, s32[4]{0:T(128)}) custom-call(s32[1,1]{1,0:T(1,128)S(6)} %copy.12.count_ref, s32[368]{0:T(512)} %get-tuple-element.91.part_ref, s32[368]{0:T(512)} %get-tuple-element.90.entry_ref, s32[368]{0:T(512)} %get-tuple-element.89.back_ref), custom_call_target="tpu_custom_call" | custom-call | tf_op jit(solution)/shard_map/bins/pallas_call | solution.py:122
  34.3 6.5 %forward_send.2 = bf16[8192,128]{1,0:T(8,128)(2,1)} custom-call(s32[1536]{0:T(1024)} %get-tuple-element.52.list_ref, s32[4]{0:T(128)} %get-tuple-element.48.number_ref, bf16[1024,128]{1,0:T(8,128)(2,1)} %refs_0_.7, bf16[1024,128]{1,0:T(8,128)(2,1)} %collective-permute-done.1.refs_1_, bf16[1024,128]{1,0:T(8,128)(2,1)} %collective-permute-done.3.refs_2_, ...), custom_call_target="tpu_custom_call" | custom-call | tf_op jit(solution)/shard_map/forward_send/pallas_call | solution.py:287
  43.9 6.3 %forward_send.3 = bf16[8192,128]{1,0:T(8,128)(2,1)} custom-call(s32[1536]{0:T(1024)} %get-tuple-element.52.list_ref, s32[4]{0:T(128)} %get-tuple-element.48.number_ref, bf16[1024,128]{1,0:T(8,128)(2,1)} %refs_0_.7, bf16[1024,128]{1,0:T(8,128)(2,1)} %collective-permute-done.1.refs_1_, bf16[1024,128]{1,0:T(8,128)(2,1)} %collective-permute-done.3.refs_2_, ...), custom_call_target="tpu_custom_call" | custom-call | tf_op jit(solution)/shard_map/forward_send/pallas_call | solution.py:287
  51.0 6.7 %forward_keep.2 = (f32[2048,128]{1,0:T(8,128)}, bf16[2048,128]{1,0:T(8,128)(2,1)}, bf16[2048,128]{1,0:T(8,128)(2,1)}, f32[1024,128]{1,0:T(8,128)}, f32[1024,128]{1,0:T(8,128)}) custom-call(s32[1536]{0:T(1024)} %get-tuple-element.52.list_ref, s32[4]{0:T(128)} %get-tuple-element.48.number_ref, bf16[1024,128]{1,0:T(8,128)(2,1)} %refs_0_.7, ...), custom_call_target="tpu_custom_call" | custom-call | tf_op jit(solution)/shard_map/forward_keep/pallas_call | solution.py:299
  59.6 6.8 %forward_keep.3 = (f32[2048,128]{1,0:T(8,128)}, bf16[2048,128]{1,0:T(8,128)(2,1)}, bf16[2048,128]{1,0:T(8,128)(2,1)}, bf16[2048,128]{1,0:T(8,128)(2,1)}) custom-call(s32[1536]{0:T(1024)} %get-tuple-element.52.list_ref, s32[4]{0:T(128)} %get-tuple-element.48.number_ref, bf16[1024,128]{1,0:T(8,128)(2,1)} %refs_0_.7, ...), custom_call_target="tpu_custom_call" | custom-call | tf_op jit(solution)/shard_map/forward_keep/pallas_call | solution.py:299
  78.5 23.1 %collective-permute-done.11.refs_3_ = bf16[1024,128]{1,0:T(8,128)(2,1)} collective-permute-done((bf16[1024,128]{1,0:T(8,128)(2,1)}, bf16[1024,128]{1,0:T(8,128)(2,1)}, u32[]{:S(2)}, u32[]{:S(2)}) %collective-permute-start.11) | collective-permute-done | bytes 262176 | tf_op jit(solution)/shard_map/ppermute | solution.py:53
  104.1 3.8 %collective-permute-start.16 = (bf16[512,128]{1,0:T(8,128)(2,1)}, bf16[512,128]{1,0:T(8,128)(2,1)}, u32[]{:S(2)}, u32[]{:S(2)}) collective-permute-start(bf16[512,128]{1,0:T(8,128)(2,1)} %get-tuple-element.69), channel_id=1, source_target_pairs={{0,2},{1,3},{2,4},{3,5},{4,6},{5,7},{6,0},{7,1},{8,10},{9,11},{10,... | collective-permute-start | bytes 393224 | tf_op jit(solution)/shard_map/ppermute | solution.py:53
  107.9 7.1 %collective-permute-start.17 = (bf16[512,128]{1,0:T(8,128)(2,1)}, bf16[512,128]{1,0:T(8,128)(2,1)}, u32[]{:S(2)}, u32[]{:S(2)}) collective-permute-start(bf16[512,128]{1,0:T(8,128)(2,1)} %get-tuple-element.70), channel_id=1, source_target_pairs={{0,4},{1,5},{2,6},{3,7},{4,0},{5,1},{6,2},{7,3},{8,12},{9,13},{10,... | collective-permute-start | bytes 393224 | tf_op jit(solution)/shard_map/ppermute | solution.py:53
  120.9 3.5 %collective-permute-start.21 = (bf16[512,128]{1,0:T(8,128)(2,1)}, bf16[512,128]{1,0:T(8,128)(2,1)}, u32[]{:S(2)}, u32[]{:S(2)}) collective-permute-start(bf16[512,128]{1,0:T(8,128)(2,1)} %get-tuple-element.76), channel_id=1, source_target_pairs={{0,6},{1,7},{2,0},{3,1},{4,2},{5,3},{6,4},{7,5},{8,14},{9,15},{10,... | collective-permute-start | bytes 393224 | tf_op jit(solution)/shard_map/ppermute | solution.py:53
  124.4 5.1 %collective-permute-done.18.refs_3_ = bf16[512,128]{1,0:T(8,128)(2,1)} collective-permute-done((bf16[512,128]{1,0:T(8,128)(2,1)}, bf16[512,128]{1,0:T(8,128)(2,1)}, u32[]{:S(2)}, u32[]{:S(2)}) %collective-permute-start.18) | collective-permute-done | bytes 131104 | tf_op jit(solution)/shard_map/ppermute | solution.py:53
  133.2 4.0 %collective-permute-done.21.refs_3_ = bf16[512,128]{1,0:T(8,128)(2,1)} collective-permute-done((bf16[512,128]{1,0:T(8,128)(2,1)}, bf16[512,128]{1,0:T(8,128)(2,1)}, u32[]{:S(2)}, u32[]{:S(2)}) %collective-permute-start.21) | collective-permute-done | bytes 131104 | tf_op jit(solution)/shard_map/ppermute | solution.py:53
  147.9 3.3 %collective-permute-start.25 = (bf16[256,128]{1,0:T(8,128)(2,1)S(1)}, bf16[256,128]{1,0:T(8,128)(2,1)}, u32[]{:S(2)}, u32[]{:S(2)}) collective-permute-start(bf16[256,128]{1,0:T(8,128)(2,1)S(1)} %slice.17), channel_id=1, source_target_pairs={{0,6},{1,7},{2,0},{3,1},{4,2},{5,3},{6,4},{7,5},{8,14},{9,15},{10,... | collective-permute-start | bytes 196616 | tf_op jit(solution)/shard_map/ppermute | solution.py:53
  155.1 5.1 %collective-permute-start.26 = (bf16[2048,128]{1,0:T(8,128)(2,1)}, bf16[2048,128]{1,0:T(8,128)(2,1)S(1)}, u32[]{:S(2)}, u32[]{:S(2)}) collective-permute-start(bf16[2048,128]{1,0:T(8,128)(2,1)} %join.1.refs_0_), channel_id=1, source_target_pairs={{0,24},{1,25},{2,26},{3,27},{4,28},{5,29},{6,30},{7,31},{8,0},{9,1... | collective-permute-start | bytes 1572872 | tf_op jit(solution)/shard_map/ppermute | solution.py:53
  160.2 4.0 %collective-permute-start.30 = (bf16[2048,128]{1,0:T(8,128)(2,1)}, bf16[2048,128]{1,0:T(8,128)(2,1)S(1)}, u32[]{:S(2)}, u32[]{:S(2)}) collective-permute-start(bf16[2048,128]{1,0:T(8,128)(2,1)} %join.1.refs_0_), channel_id=1, source_target_pairs={{0,1},{1,0},{2,3},{3,2},{4,5},{5,4},{6,7},{7,6},{8,9},{9,8},{10,11... | collective-permute-start | bytes 1572872 | tf_op jit(solution)/shard_map/ppermute | solution.py:53
  164.2 6.9 %collective-permute-done.27.refs_4_ = bf16[2048,128]{1,0:T(8,128)(2,1)S(1)} collective-permute-done((bf16[2048,128]{1,0:T(8,128)(2,1)}, bf16[2048,128]{1,0:T(8,128)(2,1)S(1)}, u32[]{:S(2)}, u32[]{:S(2)}) %collective-permute-start.27) | collective-permute-done | bytes 524320 | tf_op jit(solution)/shard_map/ppermute | solution.py:53
  171.5 3.7 %collective-permute-start.31 = (bf16[2048,128]{1,0:T(8,128)(2,1)S(1)}, bf16[2048,128]{1,0:T(8,128)(2,1)S(1)}, u32[]{:S(2)}, u32[]{:S(2)}) collective-permute-start(bf16[2048,128]{1,0:T(8,128)(2,1)S(1)} %collective-permute-done.26.refs_1_), channel_id=1, source_target_pairs={{0,1},{1,0},{2,3},{3,2},{4,5},{5,4},{6,7},{7,6},{8,9},{9,8},{10,11... | collective-permute-start | bytes 1572872 | tf_op jit(solution)/shard_map/ppermute | solution.py:53
  178.2 8.0 %collective-permute-start.32 = (bf16[1024,128]{1,0:T(8,128)(2,1)S(1)}, bf16[1024,128]{1,0:T(8,128)(2,1)S(1)}, u32[]{:S(2)}, u32[]{:S(2)}) collective-permute-start(bf16[1024,128]{1,0:T(8,128)(2,1)S(1)} %collective-permute-done.28.refs_2_), channel_id=1, source_target_pairs={{0,1},{1,0},{2,3},{3,2},{4,5},{5,4},{6,7},{7,6},{8,9},{9,8},{10,11... | collective-permute-start | bytes 786440 | tf_op jit(solution)/shard_map/ppermute | solution.py:53
  191.7 9.6 %backward.2.refs_2_ = f32[8192,128]{1,0:T(8,128)} custom-call(s32[1536]{0:T(1024)} %get-tuple-element.52.list_ref, s32[1536]{0:T(1024)} %get-tuple-element.79.backs_ref, s32[4]{0:T(128)} %get-tuple-element.48.number_ref, bf16[2048,128]{1,0:T(8,128)(2,1)} %join.1.refs_0_, bf16[2048,128]{1,0:T(8,128)(2,1)} %copy-done.1, bf16[1024,128]{1,0:T(8,128)(2,1)} %copy-done.7, ...), custom_call_target="tpu_custom_call" | custom-call | tf_op jit(solution)/shard_map/backward/pallas_call | solution.py:498
  201.3 3.3 %all-gather.2.cloned.1.call-done.refs_0_ = bf16[20992,128]{1,0:T(8,128)(2,1)} async-done(((bf16[656,128]{1,0:T(8,128)(2,1)}), bf16[20992,128]{1,0:T(8,128)(2,1)}) %all-gather.2.cloned.1.call-update) | async-done | bytes 5373968 | tf_op jit(solution)/shard_map/all_gather | solution.py:597
  204.6 10.2 %backward.3 = bf16[9344,128]{1,0:T(8,128)(2,1)} custom-call(s32[1536]{0:T(1024)} %get-tuple-element.52.list_ref, s32[1536]{0:T(1024)} %get-tuple-element.79.backs_ref, s32[4]{0:T(128)} %get-tuple-element.48.number_ref, bf16[20992,128]{1,0:T(8,128)(2,1)} %all-gather.2.cloned.1.call-done.refs_0_, bf16[368,128,128]{2,1,0:T(8,128)(2,1)} %bitcast.10, ...), custom_call_target="tpu_custom_call" | custom-call | tf_op jit(solution)/shard_map/backward/pallas_call | solution.py:498
  214.9 32.9 %all_to_all.5 = bf16[8,1168,128]{2,1,0:T(8,128)(2,1)} all-to-all(bf16[8,1168,128]{2,1,0:T(8,128)(2,1)} %bitcast.11), channel_id=1, replica_groups=mesh['row'=8,'col'=32] {'row'}, dimensions={0} | all-to-all | bytes 4784128 | tf_op jit(solution)/shard_map/all_to_all | solution.py:603
  (94 shorter events, 69.2 us)
Async XLA Ops:
  7.2 197.5 %all-gather.2.cloned.1.call-start = ((), (), s32[]{:S(2)}) async-start(), calls=%async_computation.1 | async-start | bytes 5541888 | tf_op jit(solution)/shard_map/all_gather | solution.py:597
  18.5 12.0 %collective-permute-start.3 = (bf16[1024,128]{1,0:T(8,128)(2,1)}, bf16[1024,128]{1,0:T(8,128)(2,1)}, u32[]{:S(2)}, u32[]{:S(2)}) collective-permute-start(bf16[1024,128]{1,0:T(8,128)(2,1)} %refs_0_.7), channel_id=1, source_target_pairs={{0,192},{32,224},{64,0},{96,32},{128,64},{160,96},{192,128},{224,1... | collective-permute-start | bytes 786440 | tf_op jit(solution)/shard_map/ppermute | solution.py:49
  19.0 11.5 %collective-permute-start.6 = (bf16[1024,128]{1,0:T(8,128)(2,1)}, bf16[1024,128]{1,0:T(8,128)(2,1)}, u32[]{:S(2)}, u32[]{:S(2)}) collective-permute-start(bf16[1024,128]{1,0:T(8,128)(2,1)} %collective-permute-done.1.refs_1_), channel_id=1, source_target_pairs={{0,64},{32,96},{64,128},{96,160},{128,192},{160,224},{192,0},{224,... | collective-permute-start | bytes 786440 | tf_op jit(solution)/shard_map/ppermute | solution.py:49
  19.9 12.1 %collective-permute-start.4 = (bf16[1024,128]{1,0:T(8,128)(2,1)}, bf16[1024,128]{1,0:T(8,128)(2,1)}, u32[]{:S(2)}, u32[]{:S(2)}) collective-permute-start(bf16[1024,128]{1,0:T(8,128)(2,1)} %collective-permute-done.refs_6_), channel_id=1, source_target_pairs={{0,64},{32,96},{64,128},{96,160},{128,192},{160,224},{192,0},{224,... | collective-permute-start | bytes 786440 | tf_op jit(solution)/shard_map/ppermute | solution.py:49
  57.7 13.9 %collective-permute-start.10 = (bf16[2048,128]{1,0:T(8,128)(2,1)}, bf16[2048,128]{1,0:T(8,128)(2,1)}, u32[]{:S(2)}, u32[]{:S(2)}) collective-permute-start(bf16[2048,128]{1,0:T(8,128)(2,1)} %get-tuple-element.58), channel_id=1, source_target_pairs={{0,24},{1,25},{2,26},{3,27},{4,28},{5,29},{6,30},{7,31},{8,0},{9,1... | collective-permute-start | bytes 1572872 | tf_op jit(solution)/shard_map/ppermute | solution.py:53
  59.6 13.9 %collective-permute-start.9 = (bf16[2048,128]{1,0:T(8,128)(2,1)}, bf16[2048,128]{1,0:T(8,128)(2,1)}, u32[]{:S(2)}, u32[]{:S(2)}) collective-permute-start(bf16[2048,128]{1,0:T(8,128)(2,1)} %get-tuple-element.57), channel_id=1, source_target_pairs={{0,8},{1,9},{2,10},{3,11},{4,12},{5,13},{6,14},{7,15},{8,16},{9,17... | collective-permute-start | bytes 1572872 | tf_op jit(solution)/shard_map/ppermute | solution.py:53
  66.4 48.6 %collective-permute-start.13 = (bf16[2048,128]{1,0:T(8,128)(2,1)}, bf16[2048,128]{1,0:T(8,128)(2,1)}, u32[]{:S(2)}, u32[]{:S(2)}) collective-permute-start(bf16[2048,128]{1,0:T(8,128)(2,1)} %get-tuple-element.64), channel_id=1, source_target_pairs={{0,8},{1,9},{2,10},{3,11},{4,12},{5,13},{6,14},{7,15},{8,16},{9,17... | collective-permute-start | bytes 1572872 | tf_op jit(solution)/shard_map/ppermute | solution.py:53
  67.9 47.1 %collective-permute-start.14 = (bf16[2048,128]{1,0:T(8,128)(2,1)}, bf16[2048,128]{1,0:T(8,128)(2,1)}, u32[]{:S(2)}, u32[]{:S(2)}) collective-permute-start(bf16[2048,128]{1,0:T(8,128)(2,1)} %get-tuple-element.65), channel_id=1, source_target_pairs={{0,16},{1,17},{2,18},{3,19},{4,20},{5,21},{6,22},{7,23},{8,24},{9,... | collective-permute-start | bytes 1572872 | tf_op jit(solution)/shard_map/ppermute | solution.py:53
  69.9 45.1 %collective-permute-start.15 = (bf16[2048,128]{1,0:T(8,128)(2,1)}, bf16[2048,128]{1,0:T(8,128)(2,1)}, u32[]{:S(2)}, u32[]{:S(2)}) collective-permute-start(bf16[2048,128]{1,0:T(8,128)(2,1)} %get-tuple-element.66), channel_id=1, source_target_pairs={{0,24},{1,25},{2,26},{3,27},{4,28},{5,29},{6,30},{7,31},{8,0},{9,1... | collective-permute-start | bytes 1572872 | tf_op jit(solution)/shard_map/ppermute | solution.py:53
  75.9 25.7 %collective-permute-start.11 = (bf16[1024,128]{1,0:T(8,128)(2,1)}, bf16[1024,128]{1,0:T(8,128)(2,1)}, u32[]{:S(2)}, u32[]{:S(2)}) collective-permute-start(bf16[1024,128]{1,0:T(8,128)(2,1)} %get-tuple-element.59), channel_id=1, source_target_pairs={{0,8},{1,9},{2,10},{3,11},{4,12},{5,13},{6,14},{7,15},{8,16},{9,17... | collective-permute-start | bytes 786440 | tf_op jit(solution)/shard_map/ppermute | solution.py:53
  75.9 25.7 %collective-permute-start.12 = (bf16[1024,128]{1,0:T(8,128)(2,1)}, bf16[1024,128]{1,0:T(8,128)(2,1)}, u32[]{:S(2)}, u32[]{:S(2)}) collective-permute-start(bf16[1024,128]{1,0:T(8,128)(2,1)} %get-tuple-element.61), channel_id=1, source_target_pairs={{0,24},{1,25},{2,26},{3,27},{4,28},{5,29},{6,30},{7,31},{8,0},{9,1... | collective-permute-start | bytes 786440 | tf_op jit(solution)/shard_map/ppermute | solution.py:53
  104.1 16.8 %collective-permute-start.16 = (bf16[512,128]{1,0:T(8,128)(2,1)}, bf16[512,128]{1,0:T(8,128)(2,1)}, u32[]{:S(2)}, u32[]{:S(2)}) collective-permute-start(bf16[512,128]{1,0:T(8,128)(2,1)} %get-tuple-element.69), channel_id=1, source_target_pairs={{0,2},{1,3},{2,4},{3,5},{4,6},{5,7},{6,0},{7,1},{8,10},{9,11},{10,... | collective-permute-start | bytes 393224 | tf_op jit(solution)/shard_map/ppermute | solution.py:53
  107.9 16.5 %collective-permute-start.17 = (bf16[512,128]{1,0:T(8,128)(2,1)}, bf16[512,128]{1,0:T(8,128)(2,1)}, u32[]{:S(2)}, u32[]{:S(2)}) collective-permute-start(bf16[512,128]{1,0:T(8,128)(2,1)} %get-tuple-element.70), channel_id=1, source_target_pairs={{0,4},{1,5},{2,6},{3,7},{4,0},{5,1},{6,2},{7,3},{8,12},{9,13},{10,... | collective-permute-start | bytes 393224 | tf_op jit(solution)/shard_map/ppermute | solution.py:53
  115.0 14.6 %collective-permute-start.18 = (bf16[512,128]{1,0:T(8,128)(2,1)}, bf16[512,128]{1,0:T(8,128)(2,1)}, u32[]{:S(2)}, u32[]{:S(2)}) collective-permute-start(bf16[512,128]{1,0:T(8,128)(2,1)} %get-tuple-element.71), channel_id=1, source_target_pairs={{0,6},{1,7},{2,0},{3,1},{4,2},{5,3},{6,4},{7,5},{8,14},{9,15},{10,... | collective-permute-start | bytes 393224 | tf_op jit(solution)/shard_map/ppermute | solution.py:53
  117.6 14.4 %collective-permute-start.19 = (bf16[512,128]{1,0:T(8,128)(2,1)}, bf16[512,128]{1,0:T(8,128)(2,1)}, u32[]{:S(2)}, u32[]{:S(2)}) collective-permute-start(bf16[512,128]{1,0:T(8,128)(2,1)} %get-tuple-element.74), channel_id=1, source_target_pairs={{0,2},{1,3},{2,4},{3,5},{4,6},{5,7},{6,0},{7,1},{8,10},{9,11},{10,... | collective-permute-start | bytes 393224 | tf_op jit(solution)/shard_map/ppermute | solution.py:53
  119.9 13.3 %collective-permute-start.20 = (bf16[512,128]{1,0:T(8,128)(2,1)}, bf16[512,128]{1,0:T(8,128)(2,1)}, u32[]{:S(2)}, u32[]{:S(2)}) collective-permute-start(bf16[512,128]{1,0:T(8,128)(2,1)} %get-tuple-element.75), channel_id=1, source_target_pairs={{0,4},{1,5},{2,6},{3,7},{4,0},{5,1},{6,2},{7,3},{8,12},{9,13},{10,... | collective-permute-start | bytes 393224 | tf_op jit(solution)/shard_map/ppermute | solution.py:53
  120.9 16.4 %collective-permute-start.21 = (bf16[512,128]{1,0:T(8,128)(2,1)}, bf16[512,128]{1,0:T(8,128)(2,1)}, u32[]{:S(2)}, u32[]{:S(2)}) collective-permute-start(bf16[512,128]{1,0:T(8,128)(2,1)} %get-tuple-element.76), channel_id=1, source_target_pairs={{0,6},{1,7},{2,0},{3,1},{4,2},{5,3},{6,4},{7,5},{8,14},{9,15},{10,... | collective-permute-start | bytes 393224 | tf_op jit(solution)/shard_map/ppermute | solution.py:53
  155.1 16.0 %collective-permute-start.27 = (bf16[2048,128]{1,0:T(8,128)(2,1)}, bf16[2048,128]{1,0:T(8,128)(2,1)S(1)}, u32[]{:S(2)}, u32[]{:S(2)}) collective-permute-start(bf16[2048,128]{1,0:T(8,128)(2,1)} %join.1.refs_0_), channel_id=1, source_target_pairs={{0,8},{1,9},{2,10},{3,11},{4,12},{5,13},{6,14},{7,15},{8,16},{9,17... | collective-permute-start | bytes 1572872 | tf_op jit(solution)/shard_map/ppermute | solution.py:53
  155.1 16.4 %collective-permute-start.26 = (bf16[2048,128]{1,0:T(8,128)(2,1)}, bf16[2048,128]{1,0:T(8,128)(2,1)S(1)}, u32[]{:S(2)}, u32[]{:S(2)}) collective-permute-start(bf16[2048,128]{1,0:T(8,128)(2,1)} %join.1.refs_0_), channel_id=1, source_target_pairs={{0,24},{1,25},{2,26},{3,27},{4,28},{5,29},{6,30},{7,31},{8,0},{9,1... | collective-permute-start | bytes 1572872 | tf_op jit(solution)/shard_map/ppermute | solution.py:53
  160.2 29.3 %collective-permute-start.30 = (bf16[2048,128]{1,0:T(8,128)(2,1)}, bf16[2048,128]{1,0:T(8,128)(2,1)S(1)}, u32[]{:S(2)}, u32[]{:S(2)}) collective-permute-start(bf16[2048,128]{1,0:T(8,128)(2,1)} %join.1.refs_0_), channel_id=1, source_target_pairs={{0,1},{1,0},{2,3},{3,2},{4,5},{5,4},{6,7},{7,6},{8,9},{9,8},{10,11... | collective-permute-start | bytes 1572872 | tf_op jit(solution)/shard_map/ppermute | solution.py:53
  171.5 18.0 %collective-permute-start.31 = (bf16[2048,128]{1,0:T(8,128)(2,1)S(1)}, bf16[2048,128]{1,0:T(8,128)(2,1)S(1)}, u32[]{:S(2)}, u32[]{:S(2)}) collective-permute-start(bf16[2048,128]{1,0:T(8,128)(2,1)S(1)} %collective-permute-done.26.refs_1_), channel_id=1, source_target_pairs={{0,1},{1,0},{2,3},{3,2},{4,5},{5,4},{6,7},{7,6},{8,9},{9,8},{10,11... | collective-permute-start | bytes 1572872 | tf_op jit(solution)/shard_map/ppermute | solution.py:53
  175.2 14.4 %collective-permute-start.34 = (bf16[2048,128]{1,0:T(8,128)(2,1)S(1)}, bf16[2048,128]{1,0:T(8,128)(2,1)S(1)}, u32[]{:S(2)}, u32[]{:S(2)}) collective-permute-start(bf16[2048,128]{1,0:T(8,128)(2,1)S(1)} %collective-permute-done.27.refs_4_), channel_id=1, source_target_pairs={{0,1},{1,0},{2,3},{3,2},{4,5},{5,4},{6,7},{7,6},{8,9},{9,8},{10,11... | collective-permute-start | bytes 1572872 | tf_op jit(solution)/shard_map/ppermute | solution.py:53
  175.5 12.8 %collective-permute-start.29 = (bf16[1024,128]{1,0:T(8,128)(2,1)S(1)}, bf16[1024,128]{1,0:T(8,128)(2,1)S(1)}, u32[]{:S(2)}, u32[]{:S(2)}) collective-permute-start(bf16[1024,128]{1,0:T(8,128)(2,1)S(1)} %slice.19), channel_id=1, source_target_pairs={{0,24},{1,25},{2,26},{3,27},{4,28},{5,29},{6,30},{7,31},{8,0},{9,1... | collective-permute-start | bytes 786440 | tf_op jit(solution)/shard_map/ppermute | solution.py:53
  178.2 11.3 %collective-permute-start.32 = (bf16[1024,128]{1,0:T(8,128)(2,1)S(1)}, bf16[1024,128]{1,0:T(8,128)(2,1)S(1)}, u32[]{:S(2)}, u32[]{:S(2)}) collective-permute-start(bf16[1024,128]{1,0:T(8,128)(2,1)S(1)} %collective-permute-done.28.refs_2_), channel_id=1, source_target_pairs={{0,1},{1,0},{2,3},{3,2},{4,5},{5,4},{6,7},{7,6},{8,9},{9,8},{10,11... | collective-permute-start | bytes 786440 | tf_op jit(solution)/shard_map/ppermute | solution.py:53
  (23 other events, 134.0 us)
Sparse Core Ops, SparseCore 0:
  139.9 64.7 all-gather.1
